TPU v7x, 32 devices: a whole 2x2x4 slice. The times are simulated.
32 devices in a mesh: tok: 8 (over z, x), hid: 4 (over y, core).
Axes of the slice: x: 2, y: 2, z: 4, core: 2. Of those that a mesh axis runs over, the one named last changes fastest.
Arguments:
- inputs: float32 [1024, 4096], P('tok'), may hold values from -6 to 6
- cotangent: float32 [1024, 4096], P('tok'), may hold values from -6 to 6
- up_blocks: float32 [112, 4, 128, 128], P('hid', None, 'tok'), may hold values from -0.25 to 0.25
- down_blocks: float32 [112, 4, 128, 128], P('hid', None, 'tok'), may hold values from -0.25 to 0.25
- up_index: int32 [112, 4], P('hid'), may hold values from 0 to 31, all different within a row
- down_index: int32 [112, 4], P('hid'), may hold values from 0 to 31, all different within a row
- mom_up: float32 [112, 4, 128, 128], P('hid', None, 'tok'), may hold values from -6 to 6
- mom_down: float32 [112, 4, 128, 128], P('hid', None, 'tok'), may hold values from -6 to 6
Outputs:
- input_grad: float32 [1024, 4096], P('tok', 'hid')
- new_mom_up: float32 [112, 4, 128, 128], P('hid', None, 'tok')
- new_mom_down: float32 [112, 4, 128, 128], P('hid', None, 'tok')
Inputs may be any that keep to these rules, and one draw needn't show every extreme that they name: `up_index`: each row lists 4 different model blocks, and every model block appears in some row. `down_index`: each row lists 4 different model blocks, and every model block appears in some row.
All inputs are finite; a program needn't handle non-finite values.
Results may differ from a plain program's by a relative error of at most 0.0003.
Values sent between devices are 32-bit elements; how exact they have to be, the bound alone decides.
No kernel may reach another device: no remote copies, remote signals or barrier semaphores. Data moves between devices by JAX's collectives and lax.ppermute only.
A program may use at most 128 MiB of HBM per device.

v0:
```python
import functools

import jax
import jax.numpy as jnp
from jax import lax
from jax.experimental import pallas as pl
from jax.experimental.pallas import tpu as pltpu
from jax.sharding import PartitionSpec as P

F32, BF16 = jnp.float32, jnp.bfloat16
NN = (((1,), (0,)), ((), ()))
NT = (((1,), (1,)), ((), ()))


def swap(value, axis, bit):
    size = lax.axis_size(axis)
    return lax.ppermute(value, axis, [(i, i ^ bit) for i in range(size)])


def bits_below(size):
    return [1 << i for i in range(size.bit_length() - 1)]


def inner_size(size):
    inner = 1
    while inner * inner * 8 <= size:
        inner *= 2
    return inner


def split(value):
    high = value.astype(BF16)
    return high, (value - high.astype(F32)).astype(BF16)


def dot(a, b, dims):
    return lax.dot_general(a, b, dims, preferred_element_type=F32)


def kernel(cfg, up_at, down_at, place, *refs):
    starts, sizes, kb, blk, rows, nb, n, q, heads, first, last, awaits = cfg
    fc = sum(sizes)
    refs = list(refs)
    groups = min(n, 2)
    x_own, c_own = refs[:2]
    got, refs = refs[2:2 + heads], refs[2 + heads:]
    slabs, refs = refs[:n], refs[n:]
    prev = None
    if not first:
        prev, refs = refs[0], refs[1:]
    refs = refs[awaits:]
    grads = []
    for _ in sizes:
        grads.append(refs[:groups])
        refs = refs[groups:]
    outs, refs = refs[:4 if last else 1], refs[4 if last else 1:]
    w, xb, cb, acc, w_sem, g_sem, x_sem, i_sem = refs
    me, hid = place[0], place[1]
    span = nb // heads

    def weight_copy(r):
        start = pl.multiple_of((me ^ r) * q, q) if n > 1 else 0
        return pltpu.make_async_copy(
            slabs[r].at[:, pl.ds(starts[r], fc)], w.at[:, :, :, pl.ds(start, q), :], w_sem.at[r])

    def grad_copies(act):
        for r in range(n):
            start = pl.multiple_of((me ^ r) * q, q) if n > 1 else 0
            f0 = 0
            for p, size in enumerate(sizes):
                act(pltpu.make_async_copy(
                    w.at[:, pl.ds(f0, size), :, pl.ds(start, q), :],
                    grads[p][r % 2].at[r // 2], g_sem.at[p, r]))
                f0 += size

    def token_copies(f, slot, act):
        for k in range(kb):
            for i, (own, ats, buf) in enumerate(((x_own, up_at, xb), (c_own, down_at, cb))):
                at = ats[f * kb + k]
                col = pl.multiple_of(at * blk, blk)
                act(pltpu.make_async_copy(
                    own.at[:, pl.ds(col, blk)], buf.at[slot, k, pl.ds(0, rows)],
                    x_sem.at[slot, 4 * k + 2 * i]))
                col = pl.multiple_of(lax.rem(at, span) * blk, blk)
                holder = lax.div(at, span) ^ hid
                for r in range(heads):
                    @pl.when(holder == r)
                    def _():
                        act(pltpu.make_async_copy(
                            got[r].at[i, :, pl.ds(col, blk)],
                            buf.at[slot, k, pl.ds(rows, rows)],
                            x_sem.at[slot, 4 * k + 2 * i + 1]))

    def start(copy):
        copy.start()

    def wait(copy):
        copy.wait()

    for r in range(n):
        weight_copy(r).start()
    token_copies(0, 0, start)
    if first:
        acc[...] = jnp.zeros_like(acc)
    else:
        fill = pltpu.make_async_copy(prev, acc, i_sem.at[0])
        fill.start()
        fill.wait()
    for r in range(n):
        weight_copy(r).wait()

    def step(f, carry):
        slot = lax.rem(f, 2)

        @pl.when(f + 1 < fc)
        def _():
            token_copies(f + 1, 1 - slot, start)

        token_copies(f, slot, wait)
        xh, xl = split(jnp.concatenate([xb[slot, k] for k in range(kb)], axis=1))
        ch, cl = split(jnp.concatenate([cb[slot, k] for k in range(kb)], axis=1))
        uh, ul = split(w[0, f].reshape(kb * blk, blk))
        dh, dl = split(jnp.concatenate([w[1, f, k] for k in range(kb)], axis=1))

        wide = dot(xh, jnp.concatenate([uh, ul], axis=1), NN)
        pre = wide[:, :blk] + (wide[:, blk:] + dot(xl, uh, NN))
        wide = dot(ch, jnp.concatenate([dh, dl], axis=0), NT)
        grad_act = wide[:, :blk] + (wide[:, blk:] + dot(cl, dh, NT))
        sig = jax.nn.sigmoid(pre)
        act = pre * sig
        grad_pre = grad_act * sig * (1.0 + pre * (1.0 - sig))

        ah, al = split(act.T)
        tall = dot(jnp.concatenate([ah, al], axis=0), ch, NN)
        grad_down = tall[:blk] + (tall[blk:] + dot(ah, cl, NN))
        gh, gl = split(grad_pre.T)
        tall = dot(jnp.concatenate([gh, gl], axis=0), xh, NN)
        grad_up = tall[:blk] + (tall[blk:] + dot(gh, xl, NN))
        ph, plow = split(grad_pre)
        back = dot(jnp.concatenate([ph, plow], axis=1), jnp.concatenate([uh, uh], axis=1), NT)
        back = back + dot(ph, ul, NT)
        for k in range(kb):
            part = slice(k * blk, (k + 1) * blk)
            w[0, f, k] = grad_up[:, part].T
            w[1, f, k] = grad_down[:, part]
            at = up_at[f * kb + k]
            acc[at] = acc[at] + back[:, part]
        return carry

    lax.fori_loop(0, fc, step, 0)
    grad_copies(start)
    if last:
        copies = []
        for r in range(heads):
            for j in range(span):
                for side in range(2):
                    copies.append(pltpu.make_async_copy(
                        acc.at[(hid ^ r) * span + j, pl.ds(side * rows, rows)],
                        outs[2 * side + r % 2].at[r // 2, :, pl.ds(j * blk, blk)],
                        i_sem.at[len(copies)]))
    else:
        copies = [pltpu.make_async_copy(acc, outs[0], i_sem.at[0])]
    for copy in copies:
        copy.start()
    for copy in copies:
        copy.wait()
    grad_copies(wait)


def block_pass(x, cot, got, slabs, up_at, down_at, me, hid, tok, heads, prev, sizes, last, awaits):
    fc = up_at.shape[0]
    n = len(slabs)
    starts, parts = zip(*slabs)
    kb, q, blk = parts[0].shape[2:]
    rows, width = x.shape
    nb = width // blk
    first = prev is None
    cfg = (starts, sizes, kb, blk, rows, nb, n, q, heads, first, last, len(awaits))
    groups = min(n, 2)
    out = [jax.ShapeDtypeStruct((n // groups, 2, size, kb, q, blk), F32)
           for size in sizes for _ in range(groups)]
    if last:
        out += [jax.ShapeDtypeStruct((heads // 2, rows, width // heads), F32)] * 4
    else:
        out.append(pltpu.HBM((nb, 2 * rows, blk), F32))
    fixed = [pltpu.with_memory_space_constraint(a, pltpu.HBM)
             for a in [x, cot] + ([] if first else [prev])]
    operands = fixed[:2] + got + list(parts) + fixed[2:] + awaits
    anywhere = pl.BlockSpec(memory_space=pl.ANY)
    products = 2 * rows * fc * kb * blk * blk
    results = pl.pallas_call(
        functools.partial(kernel, cfg),
        out_shape=out,
        grid_spec=pltpu.PrefetchScalarGridSpec(
            num_scalar_prefetch=3,
            grid=(1,),
            in_specs=[anywhere] * len(operands),
            out_specs=[anywhere] * len(out),
            scratch_shapes=[
                pltpu.VMEM((2, fc, kb, blk, blk), F32),
                pltpu.VMEM((2, kb, 2 * rows, blk), F32),
                pltpu.VMEM((2, kb, 2 * rows, blk), F32),
                pltpu.VMEM((nb, 2 * rows, blk), F32),
                pltpu.SemaphoreType.DMA((n,)),
                pltpu.SemaphoreType.DMA((len(sizes), n)),
                pltpu.SemaphoreType.DMA((2, 4 * kb)),
                pltpu.SemaphoreType.DMA((2 * nb,)),
            ],
        ),
        compiler_params=pltpu.CompilerParams(vmem_limit_bytes=13 * 2**20),
        cost_estimate=pl.CostEstimate(
            flops=8 * 5 * 3 * products, bytes_accessed=16 * 2**20, transcendentals=0),
    )(up_at.reshape(-1), down_at.reshape(-1), jnp.stack([me, hid]), *operands)
    grads = []
    for p, size in enumerate(sizes):
        pair = results[p * groups:(p + 1) * groups]
        if n == 1:
            whole = pair[0].reshape(2, size, kb, tok, q // tok, blk)
            whole = jnp.take(jnp.moveaxis(whole, 3, 0), me ^ jnp.arange(tok), axis=0)
            whole = whole.reshape((tok // 2, 2) + whole.shape[1:])
            pair = whole[:, 0], whole[:, 1]
        grads.append(pair)
    return grads, results[len(sizes) * groups:]


def after(value, *others):
    return lax.optimization_barrier((value, *others))[0]


def shards(inputs, cotangent, up_blocks, down_blocks, up_index, down_index, mom_up, mom_down):
    rows, width = inputs.shape
    blocks, kb, q, blk = up_blocks.shape
    tok, heads = lax.axis_size("tok"), lax.axis_size("hid")
    me, hid = lax.axis_index("tok"), lax.axis_index("hid")
    inner = inner_size(tok)
    pair = inner
    near = bits_below(inner)
    far = [b for b in range(0, tok, 2 * inner)]
    half = blocks // 2
    cuts = [round(half * part / 14) for part in (0, 3, 7, 11, 14)]
    edges = [0, cuts[2], half]
    calls = [cuts[:2], cuts[1:3], cuts[2:]]
    side = (me // pair) % 2
    scale = (rows * tok) ** (-0.5)
    span = width // heads

    def weights(which, f0, f1):
        at = which * half + f0
        return jnp.stack([
            lax.dynamic_slice(a, (at, 0, 0, 0), (f1 - f0, kb, q, blk))
            for a in (up_blocks, down_blocks)])

    both = jnp.stack([
        lax.dynamic_slice(a, (0, hid * span), (rows, span)) for a in (inputs, cotangent)])
    tokens = swap(both, "tok", pair)
    mine, other = weights(side, 0, half), weights(1 - side, 0, half)
    most = far[-1] | pair
    parts = {0: [(0, mine)], most: [(0, swap(other, "tok", most))]}
    for bit in near:
        for r in list(parts):
            parts[r | bit] = [(0, swap(parts[r][0][1], "tok", bit))]

    pieces = {0: after(tokens, parts[most][0][1], parts[1][0][1])}
    for bit in reversed(bits_below(heads)[1:]):
        for r in list(pieces):
            pieces[r | bit] = swap(pieces[r], "hid", bit)
    pieces[1] = swap(pieces[0], "hid", 1)

    sends = [(1 - side, pair)] + [
        send for r in far if r for send in ((side, r), (1 - side, r | pair)) if send[1] != most]
    for which, to in sends:
        for r in [to] + [to | bit for bit in range(1, inner)]:
            parts[r] = []
        for f0, f1 in zip(edges[:-1], edges[1:]):
            source = weights(which, f0, f1)
            if f0:
                source = after(source, parts[to][0][1], pieces[1])
            fresh = {to: swap(source, "tok", to)}
            for bit in near:
                fresh.update({r | bit: swap(part, "tok", bit) for r, part in fresh.items()})
            for r, part in fresh.items():
                parts[r].append((f0, part))
    before = [part for r in parts if r & 1 for f0, part in parts[r] if f0]
    held = [parts[to][0][1] for _, to in sends] + [parts[most | 1][0][1]]
    for r in range(2, heads, 2):
        pieces[r | 1] = swap(after(pieces[r], *held), "hid", 1)
    got = [pieces[r] for r in range(heads)]

    mine, other = [], []

    def finish(even, got_back):
        total = even + got_back
        left = [b for b in reversed(bits_below(tok)) if b != 1]
        for bit in near[1:] + [b for b in bits_below(tok) if b > pair]:
            p = left.index(bit)
            left.remove(bit)
            total = total.reshape((2 ** p, 2, -1) + total.shape[1:])
            back = swap(total[:, 1], "tok", bit)
            total = (total[:, 0] + back).reshape((-1,) + total.shape[3:])
        folded.append(back)
        mine.append(total[0])
        other.append(swap(total[1], "tok", pair))

    partial = None
    crossed, folded = [], []
    kept = None
    for call in calls:
        f0, f1 = call[0], call[-1]
        slabs = []
        for r in range(tok):
            start, part = [(start, part) for start, part in parts[r] if start <= f0][-1]
            slabs.append((f0 - start, part))
        if q % 8:
            whole = jnp.stack([part[:, at:at + f1 - f0] for at, part in slabs])
            whole = jnp.take(whole, me ^ jnp.arange(tok), axis=0)
            slabs = [(0, jnp.moveaxis(whole, 0, 3).reshape(2, f1 - f0, kb, blk, blk))]
        at = (side * half + f0, 0)
        grads, rest = block_pass(
            inputs, cotangent, got, slabs,
            lax.dynamic_slice(up_index, at, (f1 - f0, kb)),
            lax.dynamic_slice(down_index, at, (f1 - f0, kb)),
            me, hid, tok, heads, partial,
            [b - a for a, b in zip(call[:-1], call[1:])], f1 == half,
            crossed[:1] if f1 == half else [])
        partial = rest[0]
        if kept:
            finish(kept[0], after(kept[1], partial))
            kept = None

        for even, odd in grads:
            got_back = swap(after(odd, *before, *folded[-2:-1]), "tok", 1)
            before = [got_back]
            crossed.append(got_back)
            if len(crossed) == 2:
                kept = even, got_back
                continue
            finish(even, got_back)
    shares = []
    for side_rows in range(2):
        even, odd = rest[2 * side_rows:2 * side_rows + 2]
        total = even + after(swap(odd, "hid", 1), crossed[2])
        for bit in bits_below(heads)[1:]:
            total = total.reshape((total.shape[0] // 2, 2) + total.shape[1:])
            total = total[:, 0] + swap(total[:, 1], "hid", bit)
        shares.append(total[0])
    input_grad = shares[0] + swap(shares[1], "tok", pair)

    mine, other = jnp.concatenate(mine, axis=1), jnp.concatenate(other, axis=1)
    ordered = jnp.concatenate(
        [jnp.where(side == 0, mine, other), jnp.where(side == 0, other, mine)], axis=1)
    return (
        input_grad,
        0.9 * mom_up + scale * ordered[0],
        0.9 * mom_down + scale * ordered[1],
    )


def solution(mesh):
    return jax.shard_map(
        shards,
        mesh=mesh,
        in_specs=(
            P("tok", None),
            P("tok", None),
            P("hid", None, "tok", None),
            P("hid", None, "tok", None),
            P("hid", None),
            P("hid", None),
            P("hid", None, "tok", None),
            P("hid", None, "tok", None),
        ),
        out_specs=(P("tok", "hid"), P("hid", None, "tok", None), P("hid", None, "tok", None)),
        check_vma=False,
    )
```

profile of v0, /device:TPU:0, one launch (start us, length us, event | category | flops | bytes accessed | tf_op | source)
XLA Modules:
  0.0 268.0 jit_solution(15491772149916811489)
XLA Ops:
  3.2 3.0 %collective-permute-start = (f32[2,128,1024]{2,1,0:T(8,128)}, f32[2,128,1024]{2,1,0:T(8,128)S(1)}, u32[]{:S(2)}, u32[]{:S(2)}) collective-permute-start(f32[2,128,1024]{2,1,0:T(8,128)} %pad_maximum_fusion), channel_id=1, source_target_pairs={{0,8},{4,12},{8,0},{12,4},{16,24},{20,28},{24,16},{28,20},{1,9},{5... | collective-permute-start | bytes 3145736 | tf_op jit(solution)/shard_map/ppermute | solution.py:17
  6.4 2.5 collective-permute-start.1
  9.1 1.6 collective-permute-start.2
  10.6 41.0 %collective-permute-done.1.refs_12_ = f32[2,14,4,16,128]{4,3,2,1,0:T(8,128)} collective-permute-done((f32[2,14,4,16,128]{4,3,2,1,0:T(8,128)S(1)}, f32[2,14,4,16,128]{4,3,2,1,0:T(8,128)}, u32[]{:S(2)}, u32[]{:S(2)}) %collective-permute-start.1) | collective-permute-done | bytes 917536 | tf_op jit(solution)/shard_map/ppermute | solution.py:17
  52.5 1.5 collective-permute-start.4
  54.0 1.5 collective-permute-start.7
  55.5 1.7 dynamic-slice_bitcast_fusion.6
  57.5 2.0 collective-permute-start.6
  59.5 15.0 %collective-permute-done.5.refs_8_ = f32[2,7,4,16,128]{4,3,2,1,0:T(8,128)S(1)} collective-permute-done((f32[2,7,4,16,128]{4,3,2,1,0:T(8,128)S(1)}, f32[2,7,4,16,128]{4,3,2,1,0:T(8,128)S(1)}, u32[]{:S(2)}, u32[]{:S(2)}) %collective-permute-start.5) | collective-permute-done | bytes 458784 | tf_op jit(solution)/shard_map/ppermute | solution.py:17
  74.5 6.9 %collective-permute-done.6.refs_10_ = f32[2,7,4,16,128]{4,3,2,1,0:T(8,128)} collective-permute-done((f32[2,7,4,16,128]{4,3,2,1,0:T(8,128)S(1)}, f32[2,7,4,16,128]{4,3,2,1,0:T(8,128)}, u32[]{:S(2)}, u32[]{:S(2)}) %collective-permute-start.6) | collective-permute-done | bytes 458784 | tf_op jit(solution)/shard_map/ppermute | solution.py:17
  84.1 2.2 collective-permute-start.11
  86.9 1.5 collective-permute-start.14
  89.0 17.2 %collective-permute-done.9.refs_8_ = f32[2,7,4,16,128]{4,3,2,1,0:T(8,128)} collective-permute-done((f32[2,7,4,16,128]{4,3,2,1,0:T(8,128)}, f32[2,7,4,16,128]{4,3,2,1,0:T(8,128)}, u32[]{:S(2)}, u32[]{:S(2)}) %collective-permute-start.9) | collective-permute-done | bytes 458784 | tf_op jit(solution)/shard_map/ppermute | solution.py:17
  113.2 8.7 %shard_map.103 = (f32[4,2,3,4,16,128]{5,4,3,2,1,0:T(8,128)S(1)}, f32[4,2,3,4,16,128]{5,4,3,2,1,0:T(8,128)}, f32[32,256,128]{2,1,0:T(8,128)}) custom-call(s32[12]{0:T(128)S(1)} %reshape.70.up_at, s32[12]{0:T(128)S(1)} %reshape.71.down_at, s32[2]{0:T(128)S(1)} %pad_add_fusion.place, f32[128,4096]{1,0:T(8,128)} %refs_0_.5, f32[128,4096]{1,0:T(8,128)} %refs_1_.5, ...), custom_call_target="tpu_custom_call" | custom-call | flops 6039797760 | bytes 16777216 | tf_op jit(solution)/shard_map/pallas_call | solution.py:191
  122.7 5.4 %collective-permute-done.12.refs_11_ = f32[2,7,4,16,128]{4,3,2,1,0:T(8,128)S(1)} collective-permute-done((f32[2,7,4,16,128]{4,3,2,1,0:T(8,128)}, f32[2,7,4,16,128]{4,3,2,1,0:T(8,128)S(1)}, u32[]{:S(2)}, u32[]{:S(2)}) %collective-permute-start.12) | collective-permute-done | bytes 458784 | tf_op jit(solution)/shard_map/ppermute | solution.py:17
  136.1 11.5 %shard_map.104 = (f32[4,2,4,4,16,128]{5,4,3,2,1,0:T(8,128)S(1)}, f32[4,2,4,4,16,128]{5,4,3,2,1,0:T(8,128)S(1)}, f32[32,256,128]{2,1,0:T(8,128)}) custom-call(s32[16]{0:T(128)S(1)} %reshape.68.up_at, s32[16]{0:T(128)S(1)} %reshape.69.down_at, s32[2]{0:T(128)S(1)} %pad_add_fusion.place, f32[128,4096]{1,0:T(8,128)} %refs_0_.5, f32[128,4096]{1,0:T(8,128)} %refs_1_.5, ...), custom_call_target="tpu_custom_call" | custom-call | flops 8053063680 | bytes 16777216 | tf_op jit(solution)/shard_map/pallas_call | solution.py:191
  151.5 15.4 %shard_map.105 = (f32[4,2,4,4,16,128]{5,4,3,2,1,0:T(8,128)S(1)}, f32[4,2,4,4,16,128]{5,4,3,2,1,0:T(8,128)}, f32[4,2,3,4,16,128]{5,4,3,2,1,0:T(8,128)S(1)}, f32[4...) custom-call(s32[28]{0:T(128)S(1)} %reshape.66.up_at, ...), custom_call_target="tpu_custom_call" | custom-call | flops 14092861440 | bytes 16777216 | tf_op jit(solution)/shard_map/pallas_call | solution.py:191
  166.9 5.7 %collective-permute-done.17 = f32[4,2,4,4,16,128]{5,4,3,2,1,0:T(8,128)S(1)} collective-permute-done((f32[4,2,4,4,16,128]{5,4,3,2,1,0:T(8,128)S(1)}, f32[4,2,4,4,16,128]{5,4,3,2,1,0:T(8,128)S(1)}, u32[]{:S(2)}, u32[]{:S(2)}) %collective-permute-start.17) | collective-permute-done | bytes 1048608 | tf_op jit(solution)/shard_map/ppermute | solution.py:17
  174.4 1.6 collective-permute-start.19
  177.6 19.0 %collective-permute-done.24 = f32[1,2,2,4,4,16,128]{6,5,4,3,2,1,0:T(8,128)S(1)} collective-permute-done((f32[1,2,2,4,4,16,128]{6,5,4,3,2,1,0:T(8,128)S(1)}, f32[1,2,2,4,4,16,128]{6,5,4,3,2,1,0:T(8,128)S(1)}, u32[]{:S(2)}, u32[]{:S(2)}) %collective-permute-start.24) | collective-permute-done | bytes 524320 | tf_op jit(solution)/shard_map/ppermute | solution.py:17
  198.4 7.6 %collective-permute-done.29 = f32[2,4,4,16,128]{4,3,2,1,0:T(8,128)} collective-permute-done((f32[2,4,4,16,128]{4,3,2,1,0:T(8,128)}, f32[2,4,4,16,128]{4,3,2,1,0:T(8,128)}, u32[]{:S(2)}, u32[]{:S(2)}) %collective-permute-start.29) | collective-permute-done | bytes 262176 | tf_op jit(solution)/shard_map/ppermute | solution.py:17
  206.9 1.4 add.117
  208.9 1.7 collective-permute-start.26
  214.0 1.7 collective-permute-start.22
  215.6 17.9 %collective-permute-done.25 = f32[1,2,2,4,4,16,128]{6,5,4,3,2,1,0:T(8,128)S(1)} collective-permute-done((f32[1,2,2,4,4,16,128]{6,5,4,3,2,1,0:T(8,128)S(1)}, f32[1,2,2,4,4,16,128]{6,5,4,3,2,1,0:T(8,128)S(1)}, u32[]{:S(2)}, u32[]{:S(2)}) %collective-permute-start.25) | collective-permute-done | bytes 524320 | tf_op jit(solution)/shard_map/ppermute | solution.py:17
  234.0 2.1 collective-permute-start.30
  236.2 1.5 collective-permute-start.23
  237.7 11.4 %collective-permute-done.30 = f32[2,4,4,16,128]{4,3,2,1,0:T(8,128)S(1)} collective-permute-done((f32[2,4,4,16,128]{4,3,2,1,0:T(8,128)S(1)}, f32[2,4,4,16,128]{4,3,2,1,0:T(8,128)S(1)}, u32[]{:S(2)}, u32[]{:S(2)}) %collective-permute-start.30) | collective-permute-done | bytes 262176 | tf_op jit(solution)/shard_map/ppermute | solution.py:17
  249.1 4.1 %collective-permute-done.27 = f32[1,2,2,3,4,16,128]{6,5,4,3,2,1,0:T(8,128)S(1)} collective-permute-done((f32[1,2,2,3,4,16,128]{6,5,4,3,2,1,0:T(8,128)S(1)}, f32[1,2,2,3,4,16,128]{6,5,4,3,2,1,0:T(8,128)S(1)}, u32[]{:S(2)}, u32[]{:S(2)}) %collective-permute-start.27) | collective-permute-done | bytes 393248 | tf_op jit(solution)/shard_map/ppermute | solution.py:17
  253.4 9.5 %collective-permute-done.23 = f32[128,1024]{1,0:T(8,128)S(1)} collective-permute-done((f32[128,1024]{1,0:T(8,128)S(1)}, f32[128,1024]{1,0:T(8,128)S(1)}, u32[]{:S(2)}, u32[]{:S(2)}) %collective-permute-start.23) | collective-permute-done | bytes 524320 | tf_op jit(solution)/shard_map/ppermute | solution.py:17
  263.8 2.4 collective-permute-done.31
  266.3 1.6 fusion.6
  (159 shorter events, 39.0 us)
Async XLA Ops:
  3.2 49.3 %collective-permute-start = (f32[2,128,1024]{2,1,0:T(8,128)}, f32[2,128,1024]{2,1,0:T(8,128)S(1)}, u32[]{:S(2)}, u32[]{:S(2)}) collective-permute-start(f32[2,128,1024]{2,1,0:T(8,128)} %pad_maximum_fusion), channel_id=1, source_target_pairs={{0,8},{4,12},{8,0},{12,4},{16,24},{20,28},{24,16},{28,20},{1,9},{5... | collective-permute-start | bytes 3145736 | tf_op jit(solution)/shard_map/ppermute | solution.py:17
  6.4 45.1 %collective-permute-start.1 = (f32[2,14,4,16,128]{4,3,2,1,0:T(8,128)S(1)}, f32[2,14,4,16,128]{4,3,2,1,0:T(8,128)}, u32[]{:S(2)}, u32[]{:S(2)}) collective-permute-start(f32[2,14,4,16,128]{4,3,2,1,0:T(8,128)S(1)} %pad_maximum_fusion.2), channel_id=1, source_target_pairs={{0,24},{4,28},{8,16},{12,20},{16,8},{20,12},{24,0},{28,4},{1,25},{... | collective-permute-start | bytes 2752520 | tf_op jit(solution)/shard_map/ppermute | solution.py:17
  9.1 42.5 %collective-permute-start.2 = (f32[2,14,4,16,128]{4,3,2,1,0:T(8,128)S(1)}, f32[2,14,4,16,128]{4,3,2,1,0:T(8,128)S(1)}, u32[]{:S(2)}, u32[]{:S(2)}) collective-permute-start(f32[2,14,4,16,128]{4,3,2,1,0:T(8,128)S(1)} %pad_maximum_fusion.3.refs_6_), channel_id=1, source_target_pairs={{0,4},{4,0},{8,12},{12,8},{16,20},{20,16},{24,28},{28,24},{1,5},{5... | collective-permute-start | bytes 2752520 | tf_op jit(solution)/shard_map/ppermute | solution.py:17
  52.5 28.8 %collective-permute-start.4 = (f32[2,128,1024]{2,1,0:T(8,128)S(1)}, f32[2,128,1024]{2,1,0:T(8,128)S(1)}, u32[]{:S(2)}, u32[]{:S(2)}) collective-permute-start(f32[2,128,1024]{2,1,0:T(8,128)S(1)} %collective-permute-done.refs_2_), channel_id=1, source_target_pairs={{0,2},{1,3},{2,0},{3,1},{4,6},{5,7},{6,4},{7,5},{8,10},{9,11},{10,... | collective-permute-start | bytes 3145736 | tf_op jit(solution)/shard_map/ppermute | solution.py:17
  54.0 27.3 %collective-permute-start.7 = (f32[2,14,4,16,128]{4,3,2,1,0:T(8,128)}, f32[2,14,4,16,128]{4,3,2,1,0:T(8,128)}, u32[]{:S(2)}, u32[]{:S(2)}) collective-permute-start(f32[2,14,4,16,128]{4,3,2,1,0:T(8,128)} %collective-permute-done.1.refs_12_), channel_id=1, source_target_pairs={{0,4},{4,0},{8,12},{12,8},{16,20},{20,16},{24,28},{28,24},{1,5},{5... | collective-permute-start | bytes 2752520 | tf_op jit(solution)/shard_map/ppermute | solution.py:17
  57.3 17.2 %collective-permute-start.5 = (f32[2,7,4,16,128]{4,3,2,1,0:T(8,128)S(1)}, f32[2,7,4,16,128]{4,3,2,1,0:T(8,128)S(1)}, u32[]{:S(2)}, u32[]{:S(2)}) collective-permute-start(f32[2,7,4,16,128]{4,3,2,1,0:T(8,128)S(1)} %pad_maximum_fusion.5), channel_id=1, source_target_pairs={{0,8},{4,12},{8,0},{12,4},{16,24},{20,28},{24,16},{28,20},{1,9},{5... | collective-permute-start | bytes 1376264 | tf_op jit(solution)/shard_map/ppermute | solution.py:17
  57.3 25.8 %collective-permute-start.3 = (f32[2,128,1024]{2,1,0:T(8,128)S(1)}, f32[2,128,1024]{2,1,0:T(8,128)S(1)}, u32[]{:S(2)}, u32[]{:S(2)}) collective-permute-start(f32[2,128,1024]{2,1,0:T(8,128)S(1)} %collective-permute-done.refs_2_), channel_id=1, source_target_pairs={{0,1},{1,0},{2,3},{3,2},{4,5},{5,4},{6,7},{7,6},{8,9},{9,8},{10,11... | collective-permute-start | bytes 3145736 | tf_op jit(solution)/shard_map/ppermute | solution.py:17
  57.5 23.9 %collective-permute-start.6 = (f32[2,7,4,16,128]{4,3,2,1,0:T(8,128)S(1)}, f32[2,7,4,16,128]{4,3,2,1,0:T(8,128)}, u32[]{:S(2)}, u32[]{:S(2)}) collective-permute-start(f32[2,7,4,16,128]{4,3,2,1,0:T(8,128)S(1)} %pad_maximum_fusion.6), channel_id=1, source_target_pairs={{0,16},{4,20},{8,24},{12,28},{16,0},{20,4},{24,8},{28,12},{1,17},{... | collective-permute-start | bytes 1376264 | tf_op jit(solution)/shard_map/ppermute | solution.py:17
  81.3 27.2 %collective-permute-start.8 = (f32[2,128,1024]{2,1,0:T(8,128)S(1)}, f32[2,128,1024]{2,1,0:T(8,128)}, u32[]{:S(2)}, u32[]{:S(2)}) collective-permute-start(f32[2,128,1024]{2,1,0:T(8,128)S(1)} %collective-permute-done.4.refs_4_), channel_id=1, source_target_pairs={{0,1},{1,0},{2,3},{3,2},{4,5},{5,4},{6,7},{7,6},{8,9},{9,8},{10,11... | collective-permute-start | bytes 3145736 | tf_op jit(solution)/shard_map/ppermute | solution.py:17
  84.1 22.0 %collective-permute-start.9 = (f32[2,7,4,16,128]{4,3,2,1,0:T(8,128)}, f32[2,7,4,16,128]{4,3,2,1,0:T(8,128)}, u32[]{:S(2)}, u32[]{:S(2)}) collective-permute-start(f32[2,7,4,16,128]{4,3,2,1,0:T(8,128)} %pad_maximum_fusion.7), channel_id=1, source_target_pairs={{0,8},{4,12},{8,0},{12,4},{16,24},{20,28},{24,16},{28,20},{1,9},{5... | collective-permute-start | bytes 1376264 | tf_op jit(solution)/shard_map/ppermute | solution.py:17
  84.1 23.9 %collective-permute-start.11 = (f32[2,7,4,16,128]{4,3,2,1,0:T(8,128)}, f32[2,7,4,16,128]{4,3,2,1,0:T(8,128)}, u32[]{:S(2)}, u32[]{:S(2)}) collective-permute-start(f32[2,7,4,16,128]{4,3,2,1,0:T(8,128)} %pad_maximum_fusion.8), channel_id=1, source_target_pairs={{0,16},{4,20},{8,24},{12,28},{16,0},{20,4},{24,8},{28,12},{1,17},{... | collective-permute-start | bytes 1376264 | tf_op jit(solution)/shard_map/ppermute | solution.py:17
  86.4 22.2 %collective-permute-start.13 = (f32[2,7,4,16,128]{4,3,2,1,0:T(8,128)S(1)}, f32[2,7,4,16,128]{4,3,2,1,0:T(8,128)}, u32[]{:S(2)}, u32[]{:S(2)}) collective-permute-start(f32[2,7,4,16,128]{4,3,2,1,0:T(8,128)S(1)} %collective-permute-done.5.refs_8_), channel_id=1, source_target_pairs={{0,4},{4,0},{8,12},{12,8},{16,20},{20,16},{24,28},{28,24},{1,5},{5... | collective-permute-start | bytes 1376264 | tf_op jit(solution)/shard_map/ppermute | solution.py:17
  86.9 21.6 %collective-permute-start.14 = (f32[2,7,4,16,128]{4,3,2,1,0:T(8,128)}, f32[2,7,4,16,128]{4,3,2,1,0:T(8,128)}, u32[]{:S(2)}, u32[]{:S(2)}) collective-permute-start(f32[2,7,4,16,128]{4,3,2,1,0:T(8,128)} %collective-permute-done.6.refs_10_), channel_id=1, source_target_pairs={{0,4},{4,0},{8,12},{12,8},{16,20},{20,16},{24,28},{28,24},{1,5},{5... | collective-permute-start | bytes 1376264 | tf_op jit(solution)/shard_map/ppermute | solution.py:17
  106.1 15.8 %collective-permute-start.10 = (f32[2,7,4,16,128]{4,3,2,1,0:T(8,128)}, f32[2,7,4,16,128]{4,3,2,1,0:T(8,128)S(1)}, u32[]{:S(2)}, u32[]{:S(2)}) collective-permute-start(f32[2,7,4,16,128]{4,3,2,1,0:T(8,128)} %collective-permute-done.9.refs_8_), channel_id=1, source_target_pairs={{0,4},{4,0},{8,12},{12,8},{16,20},{20,16},{24,28},{28,24},{1,5},{5... | collective-permute-start | bytes 1376264 | tf_op jit(solution)/shard_map/ppermute | solution.py:17
  108.0 20.2 %collective-permute-start.12 = (f32[2,7,4,16,128]{4,3,2,1,0:T(8,128)}, f32[2,7,4,16,128]{4,3,2,1,0:T(8,128)S(1)}, u32[]{:S(2)}, u32[]{:S(2)}) collective-permute-start(f32[2,7,4,16,128]{4,3,2,1,0:T(8,128)} %collective-permute-done.11.refs_10_), channel_id=1, source_target_pairs={{0,4},{4,0},{8,12},{12,8},{16,20},{20,16},{24,28},{28,24},{1,5},{5... | collective-permute-start | bytes 1376264 | tf_op jit(solution)/shard_map/ppermute | solution.py:17
  128.9 18.8 %collective-permute-start.15 = (f32[4,2,3,4,16,128]{5,4,3,2,1,0:T(8,128)}, f32[4,2,3,4,16,128]{5,4,3,2,1,0:T(8,128)S(1)}, u32[]{:S(2)}, u32[]{:S(2)}) collective-permute-start(f32[4,2,3,4,16,128]{5,4,3,2,1,0:T(8,128)} %get-tuple-element.35), channel_id=1, source_target_pairs={{0,4},{4,0},{8,12},{12,8},{16,20},{20,16},{24,28},{28,24},{1,5},{5... | collective-permute-start | bytes 2359304 | tf_op jit(solution)/shard_map/ppermute | solution.py:17
  147.8 26.5 %collective-permute-start.18 = (f32[1,2,2,3,4,16,128]{6,5,4,3,2,1,0:T(8,128)S(1)}, f32[1,2,2,3,4,16,128]{6,5,4,3,2,1,0:T(8,128)S(1)}, u32[]{:S(2)}, u32[]{:S(2)}) collective-permute-start(f32[1,2,2,3,4,16,128]{6,5,4,3,2,1,0:T(8,128)S(1)} %slice_bitcast_fusion.11), channel_id=1, source_target_pairs={{0,16},{4,20},{8,24},{12,28},{16,0},{20,4},{24,8},{28,12},{1,17},{... | collective-permute-start | bytes 1179656 | tf_op jit(solution)/shard_map/ppermute | solution.py:17
  149.0 23.6 %collective-permute-start.17 = (f32[4,2,4,4,16,128]{5,4,3,2,1,0:T(8,128)S(1)}, f32[4,2,4,4,16,128]{5,4,3,2,1,0:T(8,128)S(1)}, u32[]{:S(2)}, u32[]{:S(2)}) collective-permute-start(f32[4,2,4,4,16,128]{5,4,3,2,1,0:T(8,128)S(1)} %get-tuple-element.40), channel_id=1, source_target_pairs={{0,4},{4,0},{8,12},{12,8},{16,20},{20,16},{24,28},{28,24},{1,5},{5... | collective-permute-start | bytes 3145736 | tf_op jit(solution)/shard_map/ppermute | solution.py:17
  172.9 23.7 %collective-permute-start.24 = (f32[1,2,2,4,4,16,128]{6,5,4,3,2,1,0:T(8,128)S(1)}, f32[1,2,2,4,4,16,128]{6,5,4,3,2,1,0:T(8,128)S(1)}, u32[]{:S(2)}, u32[]{:S(2)}) collective-permute-start(f32[1,2,2,4,4,16,128]{6,5,4,3,2,1,0:T(8,128)S(1)} %slice_bitcast_fusion.2), channel_id=1, source_target_pairs={{0,16},{4,20},{8,24},{12,28},{16,0},{20,4},{24,8},{28,12},{1,17},{... | collective-permute-start | bytes 1572872 | tf_op jit(solution)/shard_map/ppermute | solution.py:17
  174.3 36.3 %collective-permute-start.16 = (f32[2,128,1024]{2,1,0:T(8,128)}, f32[2,128,1024]{2,1,0:T(8,128)}, u32[]{:S(2)}, u32[]{:S(2)}) collective-permute-start(f32[2,128,1024]{2,1,0:T(8,128)} %get-tuple-element.37), channel_id=1, source_target_pairs={{0,1},{1,0},{2,3},{3,2},{4,5},{5,4},{6,7},{7,6},{8,9},{9,8},{10,11... | collective-permute-start | bytes 3145736 | tf_op jit(solution)/shard_map/ppermute | solution.py:17
  174.4 32.5 %collective-permute-start.19 = (f32[4,2,4,4,16,128]{5,4,3,2,1,0:T(8,128)}, f32[4,2,4,4,16,128]{5,4,3,2,1,0:T(8,128)}, u32[]{:S(2)}, u32[]{:S(2)}) collective-permute-start(f32[4,2,4,4,16,128]{5,4,3,2,1,0:T(8,128)} %get-tuple-element.42), channel_id=1, source_target_pairs={{0,4},{4,0},{8,12},{12,8},{16,20},{20,16},{24,28},{28,24},{1,5},{5... | collective-permute-start | bytes 3145736 | tf_op jit(solution)/shard_map/ppermute | solution.py:17
  176.7 20.7 %collective-permute-start.28 = (f32[2,3,4,16,128]{4,3,2,1,0:T(8,128)}, f32[2,3,4,16,128]{4,3,2,1,0:T(8,128)}, u32[]{:S(2)}, u32[]{:S(2)}) collective-permute-start(f32[2,3,4,16,128]{4,3,2,1,0:T(8,128)} %get-tuple-element.74), channel_id=1, source_target_pairs={{0,8},{4,12},{8,0},{12,4},{16,24},{20,28},{24,16},{28,20},{1,9},{5... | collective-permute-start | bytes 589832 | tf_op jit(solution)/shard_map/ppermute | solution.py:17
  197.4 8.5 %collective-permute-start.29 = (f32[2,4,4,16,128]{4,3,2,1,0:T(8,128)}, f32[2,4,4,16,128]{4,3,2,1,0:T(8,128)}, u32[]{:S(2)}, u32[]{:S(2)}) collective-permute-start(f32[2,4,4,16,128]{4,3,2,1,0:T(8,128)} %get-tuple-element.70), channel_id=1, source_target_pairs={{0,8},{4,12},{8,0},{12,4},{16,24},{20,28},{24,16},{28,20},{1,9},{5... | collective-permute-start | bytes 786440 | tf_op jit(solution)/shard_map/ppermute | solution.py:17
  197.4 15.1 %collective-permute-start.21 = (f32[2,128,1024]{2,1,0:T(8,128)}, f32[2,128,1024]{2,1,0:T(8,128)}, u32[]{:S(2)}, u32[]{:S(2)}) collective-permute-start(f32[2,128,1024]{2,1,0:T(8,128)} %get-tuple-element.45), channel_id=1, source_target_pairs={{0,1},{1,0},{2,3},{3,2},{4,5},{5,4},{6,7},{7,6},{8,9},{9,8},{10,11... | collective-permute-start | bytes 3145736 | tf_op jit(solution)/shard_map/ppermute | solution.py:17
  208.4 25.2 %collective-permute-start.25 = (f32[1,2,2,4,4,16,128]{6,5,4,3,2,1,0:T(8,128)S(1)}, f32[1,2,2,4,4,16,128]{6,5,4,3,2,1,0:T(8,128)S(1)}, u32[]{:S(2)}, u32[]{:S(2)}) collective-permute-start(f32[1,2,2,4,4,16,128]{6,5,4,3,2,1,0:T(8,128)S(1)} %slice_bitcast_fusion), channel_id=1, source_target_pairs={{0,16},{4,20},{8,24},{12,28},{16,0},{20,4},{24,8},{28,12},{1,17},{... | collective-permute-start | bytes 1572872 | tf_op jit(solution)/shard_map/ppermute | solution.py:17
  208.9 24.8 %collective-permute-start.26 = (f32[4,2,3,4,16,128]{5,4,3,2,1,0:T(8,128)S(1)}, f32[4,2,3,4,16,128]{5,4,3,2,1,0:T(8,128)S(1)}, u32[]{:S(2)}, u32[]{:S(2)}) collective-permute-start(f32[4,2,3,4,16,128]{5,4,3,2,1,0:T(8,128)S(1)} %copy-done.20), channel_id=1, source_target_pairs={{0,4},{4,0},{8,12},{12,8},{16,20},{20,16},{24,28},{28,24},{1,5},{5... | collective-permute-start | bytes 2359304 | tf_op jit(solution)/shard_map/ppermute | solution.py:17
  212.0 41.3 %collective-permute-start.20 = (f32[1,128,1024]{2,1,0:T(8,128)S(1)}, f32[1,128,1024]{2,1,0:T(8,128)S(1)}, u32[]{:S(2)}, u32[]{:S(2)}) collective-permute-start(f32[1,128,1024]{2,1,0:T(8,128)S(1)} %slice_bitcast_fusion.6), channel_id=1, source_target_pairs={{0,2},{1,3},{2,0},{3,1},{4,6},{5,7},{6,4},{7,5},{8,10},{9,11},{10,... | collective-permute-start | bytes 1572872 | tf_op jit(solution)/shard_map/ppermute | solution.py:17
  214.0 22.1 %collective-permute-start.22 = (f32[1,128,1024]{2,1,0:T(8,128)S(1)}, f32[1,128,1024]{2,1,0:T(8,128)S(1)}, u32[]{:S(2)}, u32[]{:S(2)}) collective-permute-start(f32[1,128,1024]{2,1,0:T(8,128)S(1)} %slice_bitcast_fusion.4), channel_id=1, source_target_pairs={{0,2},{1,3},{2,0},{3,1},{4,6},{5,7},{6,4},{7,5},{8,10},{9,11},{10,... | collective-permute-start | bytes 1572872 | tf_op jit(solution)/shard_map/ppermute | solution.py:17
  233.9 19.3 %collective-permute-start.27 = (f32[1,2,2,3,4,16,128]{6,5,4,3,2,1,0:T(8,128)S(1)}, f32[1,2,2,3,4,16,128]{6,5,4,3,2,1,0:T(8,128)S(1)}, u32[]{:S(2)}, u32[]{:S(2)}) collective-permute-start(f32[1,2,2,3,4,16,128]{6,5,4,3,2,1,0:T(8,128)S(1)} %slice_bitcast_fusion.8), channel_id=1, source_target_pairs={{0,16},{4,20},{8,24},{12,28},{16,0},{20,4},{24,8},{28,12},{1,17},{... | collective-permute-start | bytes 1179656 | tf_op jit(solution)/shard_map/ppermute | solution.py:17
  234.0 15.1 %collective-permute-start.30 = (f32[2,4,4,16,128]{4,3,2,1,0:T(8,128)S(1)}, f32[2,4,4,16,128]{4,3,2,1,0:T(8,128)S(1)}, u32[]{:S(2)}, u32[]{:S(2)}) collective-permute-start(f32[2,4,4,16,128]{4,3,2,1,0:T(8,128)S(1)} %get-tuple-element.72), channel_id=1, source_target_pairs={{0,8},{4,12},{8,0},{12,4},{16,24},{20,28},{24,16},{28,20},{1,9},{5... | collective-permute-start | bytes 786440 | tf_op jit(solution)/shard_map/ppermute | solution.py:17
  236.2 26.7 %collective-permute-start.23 = (f32[128,1024]{1,0:T(8,128)S(1)}, f32[128,1024]{1,0:T(8,128)S(1)}, u32[]{:S(2)}, u32[]{:S(2)}) collective-permute-start(f32[128,1024]{1,0:T(8,128)S(1)} %fusion.12), channel_id=1, source_target_pairs={{0,8},{4,12},{8,0},{12,4},{16,24},{20,28},{24,16},{28,20},{1,9},{5... | collective-permute-start | bytes 1572872 | tf_op jit(solution)/shard_map/ppermute | solution.py:17
  253.3 12.8 %collective-permute-start.31 = (f32[2,3,4,16,128]{4,3,2,1,0:T(8,128)S(1)}, f32[2,3,4,16,128]{4,3,2,1,0:T(8,128)S(1)}, u32[]{:S(2)}, u32[]{:S(2)}) collective-permute-start(f32[2,3,4,16,128]{4,3,2,1,0:T(8,128)S(1)} %get-tuple-element.76), channel_id=1, source_target_pairs={{0,8},{4,12},{8,0},{12,4},{16,24},{20,28},{24,16},{28,20},{1,9},{5... | collective-permute-start | bytes 589832 | tf_op jit(solution)/shard_map/ppermute | solution.py:17
  (35 other events, 422.2 us)
where the time goes:
time: 269 us; the launch traced here: 268 us
  waiting for transfers between devices  164 us (61%)
  Pallas kernels  35.6 us (13%)
  starting transfers between devices  32.6 us (12%)
  local copies, waits for them, and re-layouts  23.4 us (9%)
  other arithmetic  10.7 us (4%)
    ppermute x32, waiting for transfers between devices, swap(): return lax.ppermute(value, axis, [(i, i ^ bit) for i in range(size)])  164 us
    pallas_call x3, Pallas kernels, block_pass(): pl.pallas_call(functools.partial(kernel, cfg), out_shape=out, grid_spec=p...  35.6 us
    ppermute x32, starting transfers between devices, swap(): return lax.ppermute(value, axis, [(i, i ^ bit) for i in range(size)])  32.6 us
    unnamed x73, local copies, waits for them, and re-layouts  17.1 us
  transfers between devices with their start and end apart: 32, of which 14 were waited for; matrix products, arithmetic and copies ran while one was open for 5% of the time, Pallas kernels for 13%

commit v1 on v0

--- a/solution.py
+++ b/solution.py
@@ -167,7 +167,7 @@
     grad_copies(wait)
 
 
-def block_pass(x, cot, got, slabs, up_at, down_at, me, hid, tok, heads, prev, sizes, last, awaits):
+def block_pass(x, cot, got, slabs, up_at, down_at, me, hid, tok, heads, prev, sizes, last, awaits, loose):
     fc = up_at.shape[0]
     n = len(slabs)
     starts, parts = zip(*slabs)
@@ -183,9 +183,12 @@
         out += [jax.ShapeDtypeStruct((heads // 2, rows, width // heads), F32)] * 4
     else:
         out.append(pltpu.HBM((nb, 2 * rows, blk), F32))
-    fixed = [pltpu.with_memory_space_constraint(a, pltpu.HBM)
-             for a in [x, cot] + ([] if first else [prev])]
-    operands = fixed[:2] + got + list(parts) + fixed[2:] + awaits
+    def fixed(*arrays):
+        return [pltpu.with_memory_space_constraint(a, pltpu.HBM) for a in arrays]
+
+    parts = [part if loose[r] else fixed(part)[0] for r, part in enumerate(parts)]
+    got = [a if r % 2 and r > 1 else fixed(a)[0] for r, a in enumerate(got)]
+    operands = fixed(x, cot) + got + parts + ([] if first else fixed(prev)) + awaits
     anywhere = pl.BlockSpec(memory_space=pl.ANY)
     products = 2 * rows * fc * kb * blk * blk
     results = pl.pallas_call(
@@ -286,7 +289,7 @@
         pieces[r | 1] = swap(after(pieces[r], *held), "hid", 1)
     got = [pieces[r] for r in range(heads)]
 
-    mine, other = [], []
+    mine = []
 
     def finish(even, got_back):
         total = even + got_back
@@ -298,8 +301,7 @@
             back = swap(total[:, 1], "tok", bit)
             total = (total[:, 0] + back).reshape((-1,) + total.shape[3:])
         folded.append(back)
-        mine.append(total[0])
-        other.append(swap(total[1], "tok", pair))
+        mine.append(total)
 
     partial = None
     crossed, folded = [], []
@@ -321,7 +323,8 @@
             lax.dynamic_slice(down_index, at, (f1 - f0, kb)),
             me, hid, tok, heads, partial,
             [b - a for a, b in zip(call[:-1], call[1:])], f1 == half,
-            crossed[:1] if f1 == half else [])
+            crossed[:1] if f1 == half else [],
+            [f1 < half and r & 1 and len(parts[r]) > 1 for r in range(tok)])
         partial = rest[0]
         if kept:
             finish(kept[0], after(kept[1], partial))
@@ -338,14 +341,16 @@
     shares = []
     for side_rows in range(2):
         even, odd = rest[2 * side_rows:2 * side_rows + 2]
-        total = even + after(swap(odd, "hid", 1), crossed[2])
+        total = even + after(swap(odd, "hid", 1), crossed[1])
         for bit in bits_below(heads)[1:]:
             total = total.reshape((total.shape[0] // 2, 2) + total.shape[1:])
             total = total[:, 0] + swap(total[:, 1], "hid", bit)
         shares.append(total[0])
     input_grad = shares[0] + swap(shares[1], "tok", pair)
 
-    mine, other = jnp.concatenate(mine, axis=1), jnp.concatenate(other, axis=1)
+    other = [swap(after(total[1], *crossed[p + 1:p + 2]), "tok", pair) for p, total in enumerate(mine)]
+    mine = jnp.concatenate([total[0] for total in mine], axis=1)
+    other = jnp.concatenate(other, axis=1)
     ordered = jnp.concatenate(
         [jnp.where(side == 0, mine, other), jnp.where(side == 0, other, mine)], axis=1)
     return (

time: 269 us -> 251 us (0.933)
  local copies, waits for them, and re-layouts: 23.4 us -> 13.7 us
  waiting for transfers between devices: 164 us -> 161 us
    unnamed x73 -> x63, local copies, waits for them, and re-layouts: 17.1 us -> 10.4 us
    ppermute x32, waiting for transfers between devices: 164 us -> 161 us  [swap(): return lax.ppermute(value, axis, [(i, i ^ bit) for i in range(size)])]
  transfers between devices with their start and end apart: 32 -> 32, of which waited for: 14 -> 18; matrix products, arithmetic and copies ran while one was open for 5% -> 3% of each run, Pallas kernels for 13% -> 14%
where the time goes in v1:
time: 251 us
  waiting for transfers between devices  161 us (64%)
  Pallas kernels  35 us (14%)
  starting transfers between devices  31 us (12%)
  local copies, waits for them, and re-layouts  13.7 us (5%)
  other arithmetic  8.74 us (3%)
    ppermute x32, waiting for transfers between devices, swap(): return lax.ppermute(value, axis, [(i, i ^ bit) for i in range(size)])  161 us
    pallas_call x3, Pallas kernels, block_pass(): pl.pallas_call(functools.partial(kernel, cfg), out_shape=out, grid_spec=p...  35 us
    ppermute x32, starting transfers between devices, swap(): return lax.ppermute(value, axis, [(i, i ^ bit) for i in range(size)])  31 us
    unnamed x63, local copies, waits for them, and re-layouts  10.4 us
  transfers between devices with their start and end apart: 32, of which 18 were waited for; matrix products, arithmetic and copies ran while one was open for 3% of the time, Pallas kernels for 14%

profile of v1, /device:TPU:0, one launch (start us, length us, event | category | flops | bytes accessed | tf_op | source)
XLA Modules:
  0.0 250.6 jit_solution(1328877027645384565)
XLA Ops:
  0.7 1.4 dynamic-slice_bitcast_fusion
  2.2 3.1 %collective-permute-start = (f32[2,128,1024]{2,1,0:T(8,128)S(1)}, f32[2,128,1024]{2,1,0:T(8,128)}, u32[]{:S(2)}, u32[]{:S(2)}) collective-permute-start(f32[2,128,1024]{2,1,0:T(8,128)S(1)} %pad_maximum_fusion), channel_id=1, source_target_pairs={{0,8},{4,12},{8,0},{12,4},{16,24},{20,28},{24,16},{28,20},{1,9},{5... | collective-permute-start | bytes 3145736 | tf_op jit(solution)/shard_map/ppermute | solution.py:17
  5.5 2.5 %collective-permute-start.1 = (f32[2,14,4,16,128]{4,3,2,1,0:T(8,128)S(1)}, f32[2,14,4,16,128]{4,3,2,1,0:T(8,128)}, u32[]{:S(2)}, u32[]{:S(2)}) collective-permute-start(f32[2,14,4,16,128]{4,3,2,1,0:T(8,128)S(1)} %pad_maximum_fusion.2), channel_id=1, source_target_pairs={{0,24},{4,28},{8,16},{12,20},{16,8},{20,12},{24,0},{28,4},{1,25},{... | collective-permute-start | bytes 2752520 | tf_op jit(solution)/shard_map/ppermute | solution.py:17
  8.1 1.6 collective-permute-start.2
  9.6 40.7 %collective-permute-done.1.refs_12_ = f32[2,14,4,16,128]{4,3,2,1,0:T(8,128)} collective-permute-done((f32[2,14,4,16,128]{4,3,2,1,0:T(8,128)S(1)}, f32[2,14,4,16,128]{4,3,2,1,0:T(8,128)}, u32[]{:S(2)}, u32[]{:S(2)}) %collective-permute-start.1) | collective-permute-done | bytes 917536 | tf_op jit(solution)/shard_map/ppermute | solution.py:17
  50.4 1.6 collective-permute-start.4
  52.0 1.5 collective-permute-start.7
  53.9 2.0 collective-permute-start.6
  55.9 15.1 %collective-permute-done.5.refs_8_ = f32[2,7,4,16,128]{4,3,2,1,0:T(8,128)} collective-permute-done((f32[2,7,4,16,128]{4,3,2,1,0:T(8,128)S(1)}, f32[2,7,4,16,128]{4,3,2,1,0:T(8,128)}, u32[]{:S(2)}, u32[]{:S(2)}) %collective-permute-start.5) | collective-permute-done | bytes 458784 | tf_op jit(solution)/shard_map/ppermute | solution.py:17
  71.0 6.8 %collective-permute-done.6.refs_10_ = f32[2,7,4,16,128]{4,3,2,1,0:T(8,128)} collective-permute-done((f32[2,7,4,16,128]{4,3,2,1,0:T(8,128)S(1)}, f32[2,7,4,16,128]{4,3,2,1,0:T(8,128)}, u32[]{:S(2)}, u32[]{:S(2)}) %collective-permute-start.6) | collective-permute-done | bytes 458784 | tf_op jit(solution)/shard_map/ppermute | solution.py:17
  81.4 1.5 collective-permute-start.14
  83.4 16.5 %collective-permute-done.9.refs_8_ = f32[2,7,4,16,128]{4,3,2,1,0:T(8,128)} collective-permute-done((f32[2,7,4,16,128]{4,3,2,1,0:T(8,128)}, f32[2,7,4,16,128]{4,3,2,1,0:T(8,128)}, u32[]{:S(2)}, u32[]{:S(2)}) %collective-permute-start.9) | collective-permute-done | bytes 458784 | tf_op jit(solution)/shard_map/ppermute | solution.py:17
  100.5 2.9 %collective-permute-done.11.refs_10_ = f32[2,7,4,16,128]{4,3,2,1,0:T(8,128)} collective-permute-done((f32[2,7,4,16,128]{4,3,2,1,0:T(8,128)S(1)}, f32[2,7,4,16,128]{4,3,2,1,0:T(8,128)}, u32[]{:S(2)}, u32[]{:S(2)}) %collective-permute-start.11) | collective-permute-done | bytes 458784 | tf_op jit(solution)/shard_map/ppermute | solution.py:17
  104.0 8.6 %shard_map.103 = (f32[4,2,3,4,16,128]{5,4,3,2,1,0:T(8,128)S(1)}, f32[4,2,3,4,16,128]{5,4,3,2,1,0:T(8,128)}, f32[32,256,128]{2,1,0:T(8,128)}) custom-call(s32[12]{0:T(128)S(1)} %reshape.70.up_at, s32[12]{0:T(128)S(1)} %reshape.71.down_at, s32[2]{0:T(128)S(1)} %pad_add_fusion.place, f32[128,4096]{1,0:T(8,128)} %refs_0_.5, f32[128,4096]{1,0:T(8,128)} %refs_1_.5, ...), custom_call_target="tpu_custom_call" | custom-call | flops 6039797760 | bytes 16777216 | tf_op jit(solution)/shard_map/pallas_call | solution.py:194
  113.8 9.1 %collective-permute-done.12.refs_11_ = f32[2,7,4,16,128]{4,3,2,1,0:T(8,128)S(1)} collective-permute-done((f32[2,7,4,16,128]{4,3,2,1,0:T(8,128)}, f32[2,7,4,16,128]{4,3,2,1,0:T(8,128)S(1)}, u32[]{:S(2)}, u32[]{:S(2)}) %collective-permute-start.12) | collective-permute-done | bytes 458784 | tf_op jit(solution)/shard_map/ppermute | solution.py:17
  127.6 11.4 %shard_map.104 = (f32[4,2,4,4,16,128]{5,4,3,2,1,0:T(8,128)S(1)}, f32[4,2,4,4,16,128]{5,4,3,2,1,0:T(8,128)}, f32[32,256,128]{2,1,0:T(8,128)}) custom-call(s32[16]{0:T(128)S(1)} %reshape.68.up_at, s32[16]{0:T(128)S(1)} %reshape.69.down_at, s32[2]{0:T(128)S(1)} %pad_add_fusion.place, f32[128,4096]{1,0:T(8,128)} %refs_0_.5, f32[128,4096]{1,0:T(8,128)} %refs_1_.5, ...), custom_call_target="tpu_custom_call" | custom-call | flops 8053063680 | bytes 16777216 | tf_op jit(solution)/shard_map/pallas_call | solution.py:194
  139.1 2.9 %collective-permute-done.15.refs_15_ = f32[4,2,3,4,16,128]{5,4,3,2,1,0:T(8,128)S(1)} collective-permute-done((f32[4,2,3,4,16,128]{5,4,3,2,1,0:T(8,128)}, f32[4,2,3,4,16,128]{5,4,3,2,1,0:T(8,128)S(1)}, u32[]{:S(2)}, u32[]{:S(2)}) %collective-permute-start.15) | collective-permute-done | bytes 786464 | tf_op jit(solution)/shard_map/ppermute | solution.py:17
  142.2 2.0 collective-permute-start.22
  145.8 14.9 %shard_map.105 = (f32[4,2,4,4,16,128]{5,4,3,2,1,0:T(8,128)S(1)}, f32[4,2,4,4,16,128]{5,4,3,2,1,0:T(8,128)S(1)}, f32[4,2,3,4,16,128]{5,4,3,2,1,0:T(8,128)S(1)}, f...) custom-call(s32[28]{0:T(128)S(1)} %reshape.66.up_at, ...), custom_call_target="tpu_custom_call" | custom-call | flops 14092861440 | bytes 16777216 | tf_op jit(solution)/shard_map/pallas_call | solution.py:194
  168.6 1.5 add.115
  170.1 1.5 collective-permute-start.23
  176.4 12.5 %collective-permute-done.20 = f32[1,128,1024]{2,1,0:T(8,128)S(1)} collective-permute-done((f32[1,128,1024]{2,1,0:T(8,128)S(1)}, f32[1,128,1024]{2,1,0:T(8,128)S(1)}, u32[]{:S(2)}, u32[]{:S(2)}) %collective-permute-start.20) | collective-permute-done | bytes 524320 | tf_op jit(solution)/shard_map/ppermute | solution.py:17
  189.9 5.6 %collective-permute-done.23 = f32[1,2,2,4,4,16,128]{6,5,4,3,2,1,0:T(8,128)S(1)} collective-permute-done((f32[1,2,2,4,4,16,128]{6,5,4,3,2,1,0:T(8,128)S(1)}, f32[1,2,2,4,4,16,128]{6,5,4,3,2,1,0:T(8,128)S(1)}, u32[]{:S(2)}, u32[]{:S(2)}) %collective-permute-start.23) | collective-permute-done | bytes 524320 | tf_op jit(solution)/shard_map/ppermute | solution.py:17
  195.6 1.5 collective-permute-start.26
  197.4 1.6 collective-permute-start.25
  199.0 8.3 %collective-permute-done.21 = f32[128,1024]{1,0:T(8,128)S(1)} collective-permute-done((f32[128,1024]{1,0:T(8,128)S(1)}, f32[128,1024]{1,0:T(8,128)S(1)}, u32[]{:S(2)}, u32[]{:S(2)}) %collective-permute-start.21) | collective-permute-done | bytes 524320 | tf_op jit(solution)/shard_map/ppermute | solution.py:17
  208.2 5.4 %collective-permute-done.26 = f32[4,2,3,4,16,128]{5,4,3,2,1,0:T(8,128)S(1)} collective-permute-done((f32[4,2,3,4,16,128]{5,4,3,2,1,0:T(8,128)S(1)}, f32[4,2,3,4,16,128]{5,4,3,2,1,0:T(8,128)S(1)}, u32[]{:S(2)}, u32[]{:S(2)}) %collective-permute-start.26) | collective-permute-done | bytes 786464 | tf_op jit(solution)/shard_map/ppermute | solution.py:17
  215.0 16.3 %collective-permute-done.25 = f32[1,2,2,4,4,16,128]{6,5,4,3,2,1,0:T(8,128)S(1)} collective-permute-done((f32[1,2,2,4,4,16,128]{6,5,4,3,2,1,0:T(8,128)S(1)}, f32[1,2,2,4,4,16,128]{6,5,4,3,2,1,0:T(8,128)S(1)}, u32[]{:S(2)}, u32[]{:S(2)}) %collective-permute-start.25) | collective-permute-done | bytes 524320 | tf_op jit(solution)/shard_map/ppermute | solution.py:17
  231.5 7.5 %collective-permute-done.27 = f32[1,2,2,3,4,16,128]{6,5,4,3,2,1,0:T(8,128)S(1)} collective-permute-done((f32[1,2,2,3,4,16,128]{6,5,4,3,2,1,0:T(8,128)S(1)}, f32[1,2,2,3,4,16,128]{6,5,4,3,2,1,0:T(8,128)S(1)}, u32[]{:S(2)}, u32[]{:S(2)}) %collective-permute-start.27) | collective-permute-done | bytes 393248 | tf_op jit(solution)/shard_map/ppermute | solution.py:17
  239.2 5.4 %collective-permute-done.30 = f32[2,4,4,16,128]{4,3,2,1,0:T(8,128)S(1)} collective-permute-done((f32[2,4,4,16,128]{4,3,2,1,0:T(8,128)S(1)}, f32[2,4,4,16,128]{4,3,2,1,0:T(8,128)S(1)}, u32[]{:S(2)}, u32[]{:S(2)}) %collective-permute-start.30) | collective-permute-done | bytes 262176 | tf_op jit(solution)/shard_map/ppermute | solution.py:17
  244.7 4.1 %collective-permute-done.31 = f32[2,3,4,16,128]{4,3,2,1,0:T(8,128)S(1)} collective-permute-done((f32[2,3,4,16,128]{4,3,2,1,0:T(8,128)S(1)}, f32[2,3,4,16,128]{4,3,2,1,0:T(8,128)S(1)}, u32[]{:S(2)}, u32[]{:S(2)}) %collective-permute-start.31) | collective-permute-done | bytes 196640 | tf_op jit(solution)/shard_map/ppermute | solution.py:17
  249.0 1.6 fusion.6
  (149 shorter events, 30.5 us)
Async XLA Ops:
  2.2 48.2 %collective-permute-start = (f32[2,128,1024]{2,1,0:T(8,128)S(1)}, f32[2,128,1024]{2,1,0:T(8,128)}, u32[]{:S(2)}, u32[]{:S(2)}) collective-permute-start(f32[2,128,1024]{2,1,0:T(8,128)S(1)} %pad_maximum_fusion), channel_id=1, source_target_pairs={{0,8},{4,12},{8,0},{12,4},{16,24},{20,28},{24,16},{28,20},{1,9},{5... | collective-permute-start | bytes 3145736 | tf_op jit(solution)/shard_map/ppermute | solution.py:17
  5.5 44.9 %collective-permute-start.1 = (f32[2,14,4,16,128]{4,3,2,1,0:T(8,128)S(1)}, f32[2,14,4,16,128]{4,3,2,1,0:T(8,128)}, u32[]{:S(2)}, u32[]{:S(2)}) collective-permute-start(f32[2,14,4,16,128]{4,3,2,1,0:T(8,128)S(1)} %pad_maximum_fusion.2), channel_id=1, source_target_pairs={{0,24},{4,28},{8,16},{12,20},{16,8},{20,12},{24,0},{28,4},{1,25},{... | collective-permute-start | bytes 2752520 | tf_op jit(solution)/shard_map/ppermute | solution.py:17
  8.1 42.3 %collective-permute-start.2 = (f32[2,14,4,16,128]{4,3,2,1,0:T(8,128)S(1)}, f32[2,14,4,16,128]{4,3,2,1,0:T(8,128)S(1)}, u32[]{:S(2)}, u32[]{:S(2)}) collective-permute-start(f32[2,14,4,16,128]{4,3,2,1,0:T(8,128)S(1)} %pad_maximum_fusion.3.refs_6_), channel_id=1, source_target_pairs={{0,4},{4,0},{8,12},{12,8},{16,20},{20,16},{24,28},{28,24},{1,5},{5... | collective-permute-start | bytes 2752520 | tf_op jit(solution)/shard_map/ppermute | solution.py:17
  50.4 27.3 %collective-permute-start.4 = (f32[2,128,1024]{2,1,0:T(8,128)}, f32[2,128,1024]{2,1,0:T(8,128)}, u32[]{:S(2)}, u32[]{:S(2)}) collective-permute-start(f32[2,128,1024]{2,1,0:T(8,128)} %collective-permute-done.refs_2_), channel_id=1, source_target_pairs={{0,2},{1,3},{2,0},{3,1},{4,6},{5,7},{6,4},{7,5},{8,10},{9,11},{10,... | collective-permute-start | bytes 3145736 | tf_op jit(solution)/shard_map/ppermute | solution.py:17
  52.0 25.7 %collective-permute-start.7 = (f32[2,14,4,16,128]{4,3,2,1,0:T(8,128)}, f32[2,14,4,16,128]{4,3,2,1,0:T(8,128)}, u32[]{:S(2)}, u32[]{:S(2)}) collective-permute-start(f32[2,14,4,16,128]{4,3,2,1,0:T(8,128)} %collective-permute-done.1.refs_12_), channel_id=1, source_target_pairs={{0,4},{4,0},{8,12},{12,8},{16,20},{20,16},{24,28},{28,24},{1,5},{5... | collective-permute-start | bytes 2752520 | tf_op jit(solution)/shard_map/ppermute | solution.py:17
  53.7 17.3 %collective-permute-start.5 = (f32[2,7,4,16,128]{4,3,2,1,0:T(8,128)S(1)}, f32[2,7,4,16,128]{4,3,2,1,0:T(8,128)}, u32[]{:S(2)}, u32[]{:S(2)}) collective-permute-start(f32[2,7,4,16,128]{4,3,2,1,0:T(8,128)S(1)} %pad_maximum_fusion.5), channel_id=1, source_target_pairs={{0,8},{4,12},{8,0},{12,4},{16,24},{20,28},{24,16},{28,20},{1,9},{5... | collective-permute-start | bytes 1376264 | tf_op jit(solution)/shard_map/ppermute | solution.py:17
  53.8 24.8 %collective-permute-start.3 = (f32[2,128,1024]{2,1,0:T(8,128)}, f32[2,128,1024]{2,1,0:T(8,128)S(1)}, u32[]{:S(2)}, u32[]{:S(2)}) collective-permute-start(f32[2,128,1024]{2,1,0:T(8,128)} %collective-permute-done.refs_2_), channel_id=1, source_target_pairs={{0,1},{1,0},{2,3},{3,2},{4,5},{5,4},{6,7},{7,6},{8,9},{9,8},{10,11... | collective-permute-start | bytes 3145736 | tf_op jit(solution)/shard_map/ppermute | solution.py:17
  53.9 23.9 %collective-permute-start.6 = (f32[2,7,4,16,128]{4,3,2,1,0:T(8,128)S(1)}, f32[2,7,4,16,128]{4,3,2,1,0:T(8,128)}, u32[]{:S(2)}, u32[]{:S(2)}) collective-permute-start(f32[2,7,4,16,128]{4,3,2,1,0:T(8,128)S(1)} %pad_maximum_fusion.6), channel_id=1, source_target_pairs={{0,16},{4,20},{8,24},{12,28},{16,0},{20,4},{24,8},{28,12},{1,17},{... | collective-permute-start | bytes 1376264 | tf_op jit(solution)/shard_map/ppermute | solution.py:17
  77.7 26.2 %collective-permute-start.8 = (f32[2,128,1024]{2,1,0:T(8,128)}, f32[2,128,1024]{2,1,0:T(8,128)S(1)}, u32[]{:S(2)}, u32[]{:S(2)}) collective-permute-start(f32[2,128,1024]{2,1,0:T(8,128)} %collective-permute-done.4.refs_4_), channel_id=1, source_target_pairs={{0,1},{1,0},{2,3},{3,2},{4,5},{5,4},{6,7},{7,6},{8,9},{9,8},{10,11... | collective-permute-start | bytes 3145736 | tf_op jit(solution)/shard_map/ppermute | solution.py:17
  78.6 21.4 %collective-permute-start.9 = (f32[2,7,4,16,128]{4,3,2,1,0:T(8,128)}, f32[2,7,4,16,128]{4,3,2,1,0:T(8,128)}, u32[]{:S(2)}, u32[]{:S(2)}) collective-permute-start(f32[2,7,4,16,128]{4,3,2,1,0:T(8,128)} %pad_maximum_fusion.7), channel_id=1, source_target_pairs={{0,8},{4,12},{8,0},{12,4},{16,24},{20,28},{24,16},{28,20},{1,9},{5... | collective-permute-start | bytes 1376264 | tf_op jit(solution)/shard_map/ppermute | solution.py:17
  79.6 23.8 %collective-permute-start.11 = (f32[2,7,4,16,128]{4,3,2,1,0:T(8,128)S(1)}, f32[2,7,4,16,128]{4,3,2,1,0:T(8,128)}, u32[]{:S(2)}, u32[]{:S(2)}) collective-permute-start(f32[2,7,4,16,128]{4,3,2,1,0:T(8,128)S(1)} %pad_maximum_fusion.8), channel_id=1, source_target_pairs={{0,16},{4,20},{8,24},{12,28},{16,0},{20,4},{24,8},{28,12},{1,17},{... | collective-permute-start | bytes 1376264 | tf_op jit(solution)/shard_map/ppermute | solution.py:17
  80.8 23.1 %collective-permute-start.13 = (f32[2,7,4,16,128]{4,3,2,1,0:T(8,128)}, f32[2,7,4,16,128]{4,3,2,1,0:T(8,128)S(1)}, u32[]{:S(2)}, u32[]{:S(2)}) collective-permute-start(f32[2,7,4,16,128]{4,3,2,1,0:T(8,128)} %collective-permute-done.5.refs_8_), channel_id=1, source_target_pairs={{0,4},{4,0},{8,12},{12,8},{16,20},{20,16},{24,28},{28,24},{1,5},{5... | collective-permute-start | bytes 1376264 | tf_op jit(solution)/shard_map/ppermute | solution.py:17
  81.4 22.6 %collective-permute-start.14 = (f32[2,7,4,16,128]{4,3,2,1,0:T(8,128)}, f32[2,7,4,16,128]{4,3,2,1,0:T(8,128)S(1)}, u32[]{:S(2)}, u32[]{:S(2)}) collective-permute-start(f32[2,7,4,16,128]{4,3,2,1,0:T(8,128)} %collective-permute-done.6.refs_10_), channel_id=1, source_target_pairs={{0,4},{4,0},{8,12},{12,8},{16,20},{20,16},{24,28},{28,24},{1,5},{5... | collective-permute-start | bytes 1376264 | tf_op jit(solution)/shard_map/ppermute | solution.py:17
  100.0 13.8 %collective-permute-start.10 = (f32[2,7,4,16,128]{4,3,2,1,0:T(8,128)}, f32[2,7,4,16,128]{4,3,2,1,0:T(8,128)S(1)}, u32[]{:S(2)}, u32[]{:S(2)}) collective-permute-start(f32[2,7,4,16,128]{4,3,2,1,0:T(8,128)} %collective-permute-done.9.refs_8_), channel_id=1, source_target_pairs={{0,4},{4,0},{8,12},{12,8},{16,20},{20,16},{24,28},{28,24},{1,5},{5... | collective-permute-start | bytes 1376264 | tf_op jit(solution)/shard_map/ppermute | solution.py:17
  103.4 19.5 %collective-permute-start.12 = (f32[2,7,4,16,128]{4,3,2,1,0:T(8,128)}, f32[2,7,4,16,128]{4,3,2,1,0:T(8,128)S(1)}, u32[]{:S(2)}, u32[]{:S(2)}) collective-permute-start(f32[2,7,4,16,128]{4,3,2,1,0:T(8,128)} %collective-permute-done.11.refs_10_), channel_id=1, source_target_pairs={{0,4},{4,0},{8,12},{12,8},{16,20},{20,16},{24,28},{28,24},{1,5},{5... | collective-permute-start | bytes 1376264 | tf_op jit(solution)/shard_map/ppermute | solution.py:17
  122.9 19.1 %collective-permute-start.15 = (f32[4,2,3,4,16,128]{5,4,3,2,1,0:T(8,128)}, f32[4,2,3,4,16,128]{5,4,3,2,1,0:T(8,128)S(1)}, u32[]{:S(2)}, u32[]{:S(2)}) collective-permute-start(f32[4,2,3,4,16,128]{5,4,3,2,1,0:T(8,128)} %get-tuple-element.38), channel_id=1, source_target_pairs={{0,4},{4,0},{8,12},{12,8},{16,20},{20,16},{24,28},{28,24},{1,5},{5... | collective-permute-start | bytes 2359304 | tf_op jit(solution)/shard_map/ppermute | solution.py:17
  142.2 23.8 %collective-permute-start.22 = (f32[1,2,2,3,4,16,128]{6,5,4,3,2,1,0:T(8,128)S(1)}, f32[1,2,2,3,4,16,128]{6,5,4,3,2,1,0:T(8,128)}, u32[]{:S(2)}, u32[]{:S(2)}) collective-permute-start(f32[1,2,2,3,4,16,128]{6,5,4,3,2,1,0:T(8,128)S(1)} %slice_bitcast_fusion.10), channel_id=1, source_target_pairs={{0,16},{4,20},{8,24},{12,28},{16,0},{20,4},{24,8},{28,12},{1,17},{... | collective-permute-start | bytes 1179656 | tf_op jit(solution)/shard_map/ppermute | solution.py:17
  144.1 23.6 %collective-permute-start.17 = (f32[4,2,4,4,16,128]{5,4,3,2,1,0:T(8,128)}, f32[4,2,4,4,16,128]{5,4,3,2,1,0:T(8,128)}, u32[]{:S(2)}, u32[]{:S(2)}) collective-permute-start(f32[4,2,4,4,16,128]{5,4,3,2,1,0:T(8,128)} %get-tuple-element.42), channel_id=1, source_target_pairs={{0,4},{4,0},{8,12},{12,8},{16,20},{20,16},{24,28},{28,24},{1,5},{5... | collective-permute-start | bytes 3145736 | tf_op jit(solution)/shard_map/ppermute | solution.py:17
  165.5 7.1 %collective-permute-start.19 = (f32[2,128,1024]{2,1,0:T(8,128)}, f32[2,128,1024]{2,1,0:T(8,128)}, u32[]{:S(2)}, u32[]{:S(2)}) collective-permute-start(f32[2,128,1024]{2,1,0:T(8,128)} %get-tuple-element.45), channel_id=1, source_target_pairs={{0,1},{1,0},{2,3},{3,2},{4,5},{5,4},{6,7},{7,6},{8,9},{9,8},{10,11... | collective-permute-start | bytes 3145736 | tf_op jit(solution)/shard_map/ppermute | solution.py:17
  165.5 8.6 %collective-permute-start.16 = (f32[2,128,1024]{2,1,0:T(8,128)}, f32[2,128,1024]{2,1,0:T(8,128)S(1)}, u32[]{:S(2)}, u32[]{:S(2)}) collective-permute-start(f32[2,128,1024]{2,1,0:T(8,128)} %copy-done.11), channel_id=1, source_target_pairs={{0,1},{1,0},{2,3},{3,2},{4,5},{5,4},{6,7},{7,6},{8,9},{9,8},{10,11... | collective-permute-start | bytes 3145736 | tf_op jit(solution)/shard_map/ppermute | solution.py:17
  167.7 8.7 %collective-permute-start.28 = (f32[2,3,4,16,128]{4,3,2,1,0:T(8,128)S(1)}, f32[2,3,4,16,128]{4,3,2,1,0:T(8,128)S(1)}, u32[]{:S(2)}, u32[]{:S(2)}) collective-permute-start(f32[2,3,4,16,128]{4,3,2,1,0:T(8,128)S(1)} %get-tuple-element.56), channel_id=1, source_target_pairs={{0,8},{4,12},{8,0},{12,4},{16,24},{20,28},{24,16},{28,20},{1,9},{5... | collective-permute-start | bytes 589832 | tf_op jit(solution)/shard_map/ppermute | solution.py:17
  170.1 25.3 %collective-permute-start.23 = (f32[1,2,2,4,4,16,128]{6,5,4,3,2,1,0:T(8,128)S(1)}, f32[1,2,2,4,4,16,128]{6,5,4,3,2,1,0:T(8,128)S(1)}, u32[]{:S(2)}, u32[]{:S(2)}) collective-permute-start(f32[1,2,2,4,4,16,128]{6,5,4,3,2,1,0:T(8,128)S(1)} %slice_bitcast_fusion.2), channel_id=1, source_target_pairs={{0,16},{4,20},{8,24},{12,28},{16,0},{20,4},{24,8},{28,12},{1,17},{... | collective-permute-start | bytes 1572872 | tf_op jit(solution)/shard_map/ppermute | solution.py:17
  171.6 24.0 %collective-permute-start.24 = (f32[4,2,4,4,16,128]{5,4,3,2,1,0:T(8,128)S(1)}, f32[4,2,4,4,16,128]{5,4,3,2,1,0:T(8,128)S(1)}, u32[]{:S(2)}, u32[]{:S(2)}) collective-permute-start(f32[4,2,4,4,16,128]{5,4,3,2,1,0:T(8,128)S(1)} %copy-done.10), channel_id=1, source_target_pairs={{0,4},{4,0},{8,12},{12,8},{16,20},{20,16},{24,28},{28,24},{1,5},{5... | collective-permute-start | bytes 3145736 | tf_op jit(solution)/shard_map/ppermute | solution.py:17
  174.0 14.9 %collective-permute-start.20 = (f32[1,128,1024]{2,1,0:T(8,128)S(1)}, f32[1,128,1024]{2,1,0:T(8,128)S(1)}, u32[]{:S(2)}, u32[]{:S(2)}) collective-permute-start(f32[1,128,1024]{2,1,0:T(8,128)S(1)} %slice_bitcast_fusion.4), channel_id=1, source_target_pairs={{0,2},{1,3},{2,0},{3,1},{4,6},{5,7},{6,4},{7,5},{8,10},{9,11},{10,... | collective-permute-start | bytes 1572872 | tf_op jit(solution)/shard_map/ppermute | solution.py:17
  175.2 23.8 %collective-permute-start.18 = (f32[1,128,1024]{2,1,0:T(8,128)S(1)}, f32[1,128,1024]{2,1,0:T(8,128)S(1)}, u32[]{:S(2)}, u32[]{:S(2)}) collective-permute-start(f32[1,128,1024]{2,1,0:T(8,128)S(1)} %slice_bitcast_fusion.6), channel_id=1, source_target_pairs={{0,2},{1,3},{2,0},{3,1},{4,6},{5,7},{6,4},{7,5},{8,10},{9,11},{10,... | collective-permute-start | bytes 1572872 | tf_op jit(solution)/shard_map/ppermute | solution.py:17
  189.0 18.3 %collective-permute-start.21 = (f32[128,1024]{1,0:T(8,128)S(1)}, f32[128,1024]{1,0:T(8,128)S(1)}, u32[]{:S(2)}, u32[]{:S(2)}) collective-permute-start(f32[128,1024]{1,0:T(8,128)S(1)} %fusion.12), channel_id=1, source_target_pairs={{0,8},{4,12},{8,0},{12,4},{16,24},{20,28},{24,16},{28,20},{1,9},{5... | collective-permute-start | bytes 1572872 | tf_op jit(solution)/shard_map/ppermute | solution.py:17
  195.6 18.1 %collective-permute-start.26 = (f32[4,2,3,4,16,128]{5,4,3,2,1,0:T(8,128)S(1)}, f32[4,2,3,4,16,128]{5,4,3,2,1,0:T(8,128)S(1)}, u32[]{:S(2)}, u32[]{:S(2)}) collective-permute-start(f32[4,2,3,4,16,128]{5,4,3,2,1,0:T(8,128)S(1)} %copy-done.13), channel_id=1, source_target_pairs={{0,4},{4,0},{8,12},{12,8},{16,20},{20,16},{24,28},{28,24},{1,5},{5... | collective-permute-start | bytes 2359304 | tf_op jit(solution)/shard_map/ppermute | solution.py:17
  197.4 33.9 %collective-permute-start.25 = (f32[1,2,2,4,4,16,128]{6,5,4,3,2,1,0:T(8,128)S(1)}, f32[1,2,2,4,4,16,128]{6,5,4,3,2,1,0:T(8,128)S(1)}, u32[]{:S(2)}, u32[]{:S(2)}) collective-permute-start(f32[1,2,2,4,4,16,128]{6,5,4,3,2,1,0:T(8,128)S(1)} %slice_bitcast_fusion), channel_id=1, source_target_pairs={{0,16},{4,20},{8,24},{12,28},{16,0},{20,4},{24,8},{28,12},{1,17},{... | collective-permute-start | bytes 1572872 | tf_op jit(solution)/shard_map/ppermute | solution.py:17
  208.2 31.0 %collective-permute-start.29 = (f32[2,4,4,16,128]{4,3,2,1,0:T(8,128)S(1)}, f32[2,4,4,16,128]{4,3,2,1,0:T(8,128)S(1)}, u32[]{:S(2)}, u32[]{:S(2)}) collective-permute-start(f32[2,4,4,16,128]{4,3,2,1,0:T(8,128)S(1)} %get-tuple-element.57), channel_id=1, source_target_pairs={{0,8},{4,12},{8,0},{12,4},{16,24},{20,28},{24,16},{28,20},{1,9},{5... | collective-permute-start | bytes 786440 | tf_op jit(solution)/shard_map/ppermute | solution.py:17
  213.8 25.2 %collective-permute-start.27 = (f32[1,2,2,3,4,16,128]{6,5,4,3,2,1,0:T(8,128)S(1)}, f32[1,2,2,3,4,16,128]{6,5,4,3,2,1,0:T(8,128)S(1)}, u32[]{:S(2)}, u32[]{:S(2)}) collective-permute-start(f32[1,2,2,3,4,16,128]{6,5,4,3,2,1,0:T(8,128)S(1)} %slice_bitcast_fusion.8), channel_id=1, source_target_pairs={{0,16},{4,20},{8,24},{12,28},{16,0},{20,4},{24,8},{28,12},{1,17},{... | collective-permute-start | bytes 1179656 | tf_op jit(solution)/shard_map/ppermute | solution.py:17
  231.4 13.2 %collective-permute-start.30 = (f32[2,4,4,16,128]{4,3,2,1,0:T(8,128)S(1)}, f32[2,4,4,16,128]{4,3,2,1,0:T(8,128)S(1)}, u32[]{:S(2)}, u32[]{:S(2)}) collective-permute-start(f32[2,4,4,16,128]{4,3,2,1,0:T(8,128)S(1)} %get-tuple-element.58), channel_id=1, source_target_pairs={{0,8},{4,12},{8,0},{12,4},{16,24},{20,28},{24,16},{28,20},{1,9},{5... | collective-permute-start | bytes 786440 | tf_op jit(solution)/shard_map/ppermute | solution.py:17
  239.1 9.6 %collective-permute-start.31 = (f32[2,3,4,16,128]{4,3,2,1,0:T(8,128)S(1)}, f32[2,3,4,16,128]{4,3,2,1,0:T(8,128)S(1)}, u32[]{:S(2)}, u32[]{:S(2)}) collective-permute-start(f32[2,3,4,16,128]{4,3,2,1,0:T(8,128)S(1)} %get-tuple-element.82), channel_id=1, source_target_pairs={{0,8},{4,12},{8,0},{12,4},{16,24},{20,28},{24,16},{28,20},{1,9},{5... | collective-permute-start | bytes 589832 | tf_op jit(solution)/shard_map/ppermute | solution.py:17
  (30 other events, 221.8 us)

commit v2 on v1

--- a/solution.py
+++ b/solution.py
@@ -331,8 +331,10 @@
             kept = None
 
         for even, odd in grads:
-            got_back = swap(after(odd, *before, *folded[-2:-1]), "tok", 1)
-            before = [got_back]
+            if len(crossed) > 2:
+                before = crossed[-1:]
+            got_back = swap(after(odd, *before), "tok", 1)
+            before = []
             crossed.append(got_back)
             if len(crossed) == 2:
                 kept = even, got_back

time: 251 us -> 250 us (level)
  local copies, waits for them, and re-layouts: 13.7 us -> 8.29 us
  starting transfers between devices: 31 us -> 35.3 us
    unnamed x63 -> x49, local copies, waits for them, and re-layouts: 10.4 us -> 3.4 us
    ppermute x32, starting transfers between devices: 31 us -> 35.3 us  [swap(): return lax.ppermute(value, axis, [(i, i ^ bit) for i in range(size)])]
  transfers between devices with their start and end apart: 32 -> 32, of which waited for: 18 -> 19; matrix products, arithmetic and copies ran while one was open for 3% -> 4% of each run, Pallas kernels for 14% -> 14%
where the time goes in v2:
time: 250 us; the launch traced here: 249 us
  waiting for transfers between devices  160 us (64%)
  starting transfers between devices  35.3 us (14%)
  Pallas kernels  35.1 us (14%)
  other arithmetic  9.1 us (4%)
  local copies, waits for them, and re-layouts  8.29 us (3%)
    ppermute x32, waiting for transfers between devices, swap(): return lax.ppermute(value, axis, [(i, i ^ bit) for i in range(size)])  160 us
    ppermute x32, starting transfers between devices, swap(): return lax.ppermute(value, axis, [(i, i ^ bit) for i in range(size)])  35.3 us
    pallas_call x3, Pallas kernels, block_pass(): pl.pallas_call(functools.partial(kernel, cfg), out_shape=out, grid_spec=p...  35.1 us
  transfers between devices with their start and end apart: 32, of which 19 were waited for; matrix products, arithmetic and copies ran while one was open for 4% of the time, Pallas kernels for 14%

profile of v2, /device:TPU:0, one launch (start us, length us, event | category | flops | bytes accessed | tf_op | source)
XLA Modules:
  0.0 249.1 jit_solution(5148204665799816754)
XLA Ops:
  2.2 3.1 %collective-permute-start = (f32[2,128,1024]{2,1,0:T(8,128)S(1)}, f32[2,128,1024]{2,1,0:T(8,128)}, u32[]{:S(2)}, u32[]{:S(2)}) collective-permute-start(f32[2,128,1024]{2,1,0:T(8,128)S(1)} %pad_maximum_fusion), channel_id=1, source_target_pairs={{0,8},{4,12},{8,0},{12,4},{16,24},{20,28},{24,16},{28,20},{1,9},{5... | collective-permute-start | bytes 3145736 | tf_op jit(solution)/shard_map/ppermute | solution.py:17
  5.5 2.5 %collective-permute-start.1 = (f32[2,14,4,16,128]{4,3,2,1,0:T(8,128)S(1)}, f32[2,14,4,16,128]{4,3,2,1,0:T(8,128)}, u32[]{:S(2)}, u32[]{:S(2)}) collective-permute-start(f32[2,14,4,16,128]{4,3,2,1,0:T(8,128)S(1)} %pad_maximum_fusion.2), channel_id=1, source_target_pairs={{0,24},{4,28},{8,16},{12,20},{16,8},{20,12},{24,0},{28,4},{1,25},{... | collective-permute-start | bytes 2752520 | tf_op jit(solution)/shard_map/ppermute | solution.py:17
  8.1 1.6 collective-permute-start.2
  9.6 40.7 %collective-permute-done.1.refs_12_ = f32[2,14,4,16,128]{4,3,2,1,0:T(8,128)} collective-permute-done((f32[2,14,4,16,128]{4,3,2,1,0:T(8,128)S(1)}, f32[2,14,4,16,128]{4,3,2,1,0:T(8,128)}, u32[]{:S(2)}, u32[]{:S(2)}) %collective-permute-start.1) | collective-permute-done | bytes 917536 | tf_op jit(solution)/shard_map/ppermute | solution.py:17
  50.4 1.6 collective-permute-start.4
  52.0 1.5 collective-permute-start.7
  53.9 2.0 collective-permute-start.6
  55.9 15.1 %collective-permute-done.5.refs_8_ = f32[2,7,4,16,128]{4,3,2,1,0:T(8,128)} collective-permute-done((f32[2,7,4,16,128]{4,3,2,1,0:T(8,128)S(1)}, f32[2,7,4,16,128]{4,3,2,1,0:T(8,128)}, u32[]{:S(2)}, u32[]{:S(2)}) %collective-permute-start.5) | collective-permute-done | bytes 458784 | tf_op jit(solution)/shard_map/ppermute | solution.py:17
  71.0 6.8 %collective-permute-done.6.refs_10_ = f32[2,7,4,16,128]{4,3,2,1,0:T(8,128)} collective-permute-done((f32[2,7,4,16,128]{4,3,2,1,0:T(8,128)S(1)}, f32[2,7,4,16,128]{4,3,2,1,0:T(8,128)}, u32[]{:S(2)}, u32[]{:S(2)}) %collective-permute-start.6) | collective-permute-done | bytes 458784 | tf_op jit(solution)/shard_map/ppermute | solution.py:17
  78.9 2.2 collective-permute-start.11
  81.6 1.5 collective-permute-start.14
  83.7 17.0 %collective-permute-done.9.refs_8_ = f32[2,7,4,16,128]{4,3,2,1,0:T(8,128)} collective-permute-done((f32[2,7,4,16,128]{4,3,2,1,0:T(8,128)S(1)}, f32[2,7,4,16,128]{4,3,2,1,0:T(8,128)}, u32[]{:S(2)}, u32[]{:S(2)}) %collective-permute-start.9) | collective-permute-done | bytes 458784 | tf_op jit(solution)/shard_map/ppermute | solution.py:17
  103.7 8.6 %shard_map.103 = (f32[4,2,3,4,16,128]{5,4,3,2,1,0:T(8,128)S(1)}, f32[4,2,3,4,16,128]{5,4,3,2,1,0:T(8,128)}, f32[32,256,128]{2,1,0:T(8,128)}) custom-call(s32[12]{0:T(128)S(1)} %reshape.70.up_at, s32[12]{0:T(128)S(1)} %reshape.71.down_at, s32[2]{0:T(128)S(1)} %pad_add_fusion.place, f32[128,4096]{1,0:T(8,128)} %refs_0_.5, f32[128,4096]{1,0:T(8,128)} %refs_1_.5, ...), custom_call_target="tpu_custom_call" | custom-call | flops 6039797760 | bytes 16777216 | tf_op jit(solution)/shard_map/pallas_call | solution.py:194
  112.3 2.1 collective-permute-done.10.refs_9_
  114.3 8.8 %collective-permute-done.12.refs_11_ = f32[2,7,4,16,128]{4,3,2,1,0:T(8,128)S(1)} collective-permute-done((f32[2,7,4,16,128]{4,3,2,1,0:T(8,128)}, f32[2,7,4,16,128]{4,3,2,1,0:T(8,128)S(1)}, u32[]{:S(2)}, u32[]{:S(2)}) %collective-permute-start.12) | collective-permute-done | bytes 458784 | tf_op jit(solution)/shard_map/ppermute | solution.py:17
  125.7 11.2 %shard_map.104 = (f32[4,2,4,4,16,128]{5,4,3,2,1,0:T(8,128)S(1)}, f32[4,2,4,4,16,128]{5,4,3,2,1,0:T(8,128)S(1)}, f32[32,256,128]{2,1,0:T(8,128)}) custom-call(s32[16]{0:T(128)S(1)} %reshape.68.up_at, s32[16]{0:T(128)S(1)} %reshape.69.down_at, s32[2]{0:T(128)S(1)} %pad_add_fusion.place, f32[128,4096]{1,0:T(8,128)} %refs_0_.5, f32[128,4096]{1,0:T(8,128)} %refs_1_.5, ...), custom_call_target="tpu_custom_call" | custom-call | flops 8053063680 | bytes 16777216 | tf_op jit(solution)/shard_map/pallas_call | solution.py:194
  138.3 5.5 %collective-permute-done.15.refs_15_ = f32[4,2,3,4,16,128]{5,4,3,2,1,0:T(8,128)S(1)} collective-permute-done((f32[4,2,3,4,16,128]{5,4,3,2,1,0:T(8,128)}, f32[4,2,3,4,16,128]{5,4,3,2,1,0:T(8,128)S(1)}, u32[]{:S(2)}, u32[]{:S(2)}) %collective-permute-start.15) | collective-permute-done | bytes 786464 | tf_op jit(solution)/shard_map/ppermute | solution.py:17
  146.2 15.2 %shard_map.105 = (f32[4,2,4,4,16,128]{5,4,3,2,1,0:T(8,128)S(1)}, f32[4,2,4,4,16,128]{5,4,3,2,1,0:T(8,128)}, f32[4,2,3,4,16,128]{5,4,3,2,1,0:T(8,128)S(1)}, f32[4...) custom-call(s32[28]{0:T(128)S(1)} %reshape.66.up_at, ...), custom_call_target="tpu_custom_call" | custom-call | flops 14092861440 | bytes 16777216 | tf_op jit(solution)/shard_map/pallas_call | solution.py:194
  162.1 4.2 %collective-permute-done.17 = f32[4,2,4,4,16,128]{5,4,3,2,1,0:T(8,128)S(1)} collective-permute-done((f32[4,2,4,4,16,128]{5,4,3,2,1,0:T(8,128)S(1)}, f32[4,2,4,4,16,128]{5,4,3,2,1,0:T(8,128)S(1)}, u32[]{:S(2)}, u32[]{:S(2)}) %collective-permute-start.17) | collective-permute-done | bytes 1048608 | tf_op jit(solution)/shard_map/ppermute | solution.py:17
  169.3 1.7 collective-permute-start.28
  171.4 9.8 %collective-permute-done.28 = f32[2,3,4,16,128]{4,3,2,1,0:T(8,128)S(1)} collective-permute-done((f32[2,3,4,16,128]{4,3,2,1,0:T(8,128)}, f32[2,3,4,16,128]{4,3,2,1,0:T(8,128)S(1)}, u32[]{:S(2)}, u32[]{:S(2)}) %collective-permute-start.28) | collective-permute-done | bytes 196640 | tf_op jit(solution)/shard_map/ppermute | solution.py:17
  181.3 8.6 %collective-permute-done.23 = f32[1,2,2,4,4,16,128]{6,5,4,3,2,1,0:T(8,128)} collective-permute-done((f32[1,2,2,4,4,16,128]{6,5,4,3,2,1,0:T(8,128)}, f32[1,2,2,4,4,16,128]{6,5,4,3,2,1,0:T(8,128)}, u32[]{:S(2)}, u32[]{:S(2)}) %collective-permute-start.23) | collective-permute-done | bytes 524320 | tf_op jit(solution)/shard_map/ppermute | solution.py:17
  194.9 2.7 %collective-permute-start.29 = (f32[2,4,4,16,128]{4,3,2,1,0:T(8,128)S(1)}, f32[2,4,4,16,128]{4,3,2,1,0:T(8,128)S(1)}, u32[]{:S(2)}, u32[]{:S(2)}) collective-permute-start(f32[2,4,4,16,128]{4,3,2,1,0:T(8,128)S(1)} %get-tuple-element.53), channel_id=1, source_target_pairs={{0,8},{4,12},{8,0},{12,4},{16,24},{20,28},{24,16},{28,20},{1,9},{5... | collective-permute-start | bytes 786440 | tf_op jit(solution)/shard_map/ppermute | solution.py:17
  201.1 8.5 %collective-permute-done.29 = f32[2,4,4,16,128]{4,3,2,1,0:T(8,128)S(1)} collective-permute-done((f32[2,4,4,16,128]{4,3,2,1,0:T(8,128)S(1)}, f32[2,4,4,16,128]{4,3,2,1,0:T(8,128)S(1)}, u32[]{:S(2)}, u32[]{:S(2)}) %collective-permute-start.29) | collective-permute-done | bytes 262176 | tf_op jit(solution)/shard_map/ppermute | solution.py:17
  209.6 2.8 %collective-permute-done.20 = f32[1,128,1024]{2,1,0:T(8,128)S(1)} collective-permute-done((f32[1,128,1024]{2,1,0:T(8,128)S(1)}, f32[1,128,1024]{2,1,0:T(8,128)S(1)}, u32[]{:S(2)}, u32[]{:S(2)}) %collective-permute-start.20) | collective-permute-done | bytes 524320 | tf_op jit(solution)/shard_map/ppermute | solution.py:17
  212.8 2.2 collective-permute-start.27
  215.0 3.0 %collective-permute-done.25 = f32[1,2,2,4,4,16,128]{6,5,4,3,2,1,0:T(8,128)S(1)} collective-permute-done((f32[1,2,2,4,4,16,128]{6,5,4,3,2,1,0:T(8,128)S(1)}, f32[1,2,2,4,4,16,128]{6,5,4,3,2,1,0:T(8,128)S(1)}, u32[]{:S(2)}, u32[]{:S(2)}) %collective-permute-start.25) | collective-permute-done | bytes 524320 | tf_op jit(solution)/shard_map/ppermute | solution.py:17
  218.2 15.5 %collective-permute-done.27 = f32[1,2,2,3,4,16,128]{6,5,4,3,2,1,0:T(8,128)S(1)} collective-permute-done((f32[1,2,2,3,4,16,128]{6,5,4,3,2,1,0:T(8,128)S(1)}, f32[1,2,2,3,4,16,128]{6,5,4,3,2,1,0:T(8,128)S(1)}, u32[]{:S(2)}, u32[]{:S(2)}) %collective-permute-start.27) | collective-permute-done | bytes 393248 | tf_op jit(solution)/shard_map/ppermute | solution.py:17
  233.7 2.7 %collective-permute-start.31 = (f32[2,3,4,16,128]{4,3,2,1,0:T(8,128)S(1)}, f32[2,3,4,16,128]{4,3,2,1,0:T(8,128)S(1)}, u32[]{:S(2)}, u32[]{:S(2)}) collective-permute-start(f32[2,3,4,16,128]{4,3,2,1,0:T(8,128)S(1)} %get-tuple-element.78), channel_id=1, source_target_pairs={{0,8},{4,12},{8,0},{12,4},{16,24},{20,28},{24,16},{28,20},{1,9},{5... | collective-permute-start | bytes 589832 | tf_op jit(solution)/shard_map/ppermute | solution.py:17
  238.4 4.7 %collective-permute-done.30 = f32[2,4,4,16,128]{4,3,2,1,0:T(8,128)S(1)} collective-permute-done((f32[2,4,4,16,128]{4,3,2,1,0:T(8,128)S(1)}, f32[2,4,4,16,128]{4,3,2,1,0:T(8,128)S(1)}, u32[]{:S(2)}, u32[]{:S(2)}) %collective-permute-start.30) | collective-permute-done | bytes 262176 | tf_op jit(solution)/shard_map/ppermute | solution.py:17
  243.2 4.1 %collective-permute-done.31 = f32[2,3,4,16,128]{4,3,2,1,0:T(8,128)S(1)} collective-permute-done((f32[2,3,4,16,128]{4,3,2,1,0:T(8,128)S(1)}, f32[2,3,4,16,128]{4,3,2,1,0:T(8,128)S(1)}, u32[]{:S(2)}, u32[]{:S(2)}) %collective-permute-start.31) | collective-permute-done | bytes 196640 | tf_op jit(solution)/shard_map/ppermute | solution.py:17
  247.5 1.6 fusion.6
  (135 shorter events, 28.8 us)
Async XLA Ops:
  2.2 48.2 %collective-permute-start = (f32[2,128,1024]{2,1,0:T(8,128)S(1)}, f32[2,128,1024]{2,1,0:T(8,128)}, u32[]{:S(2)}, u32[]{:S(2)}) collective-permute-start(f32[2,128,1024]{2,1,0:T(8,128)S(1)} %pad_maximum_fusion), channel_id=1, source_target_pairs={{0,8},{4,12},{8,0},{12,4},{16,24},{20,28},{24,16},{28,20},{1,9},{5... | collective-permute-start | bytes 3145736 | tf_op jit(solution)/shard_map/ppermute | solution.py:17
  5.5 44.9 %collective-permute-start.1 = (f32[2,14,4,16,128]{4,3,2,1,0:T(8,128)S(1)}, f32[2,14,4,16,128]{4,3,2,1,0:T(8,128)}, u32[]{:S(2)}, u32[]{:S(2)}) collective-permute-start(f32[2,14,4,16,128]{4,3,2,1,0:T(8,128)S(1)} %pad_maximum_fusion.2), channel_id=1, source_target_pairs={{0,24},{4,28},{8,16},{12,20},{16,8},{20,12},{24,0},{28,4},{1,25},{... | collective-permute-start | bytes 2752520 | tf_op jit(solution)/shard_map/ppermute | solution.py:17
  8.1 42.3 %collective-permute-start.2 = (f32[2,14,4,16,128]{4,3,2,1,0:T(8,128)S(1)}, f32[2,14,4,16,128]{4,3,2,1,0:T(8,128)S(1)}, u32[]{:S(2)}, u32[]{:S(2)}) collective-permute-start(f32[2,14,4,16,128]{4,3,2,1,0:T(8,128)S(1)} %pad_maximum_fusion.3.refs_6_), channel_id=1, source_target_pairs={{0,4},{4,0},{8,12},{12,8},{16,20},{20,16},{24,28},{28,24},{1,5},{5... | collective-permute-start | bytes 2752520 | tf_op jit(solution)/shard_map/ppermute | solution.py:17
  50.4 28.3 %collective-permute-start.4 = (f32[2,128,1024]{2,1,0:T(8,128)}, f32[2,128,1024]{2,1,0:T(8,128)}, u32[]{:S(2)}, u32[]{:S(2)}) collective-permute-start(f32[2,128,1024]{2,1,0:T(8,128)} %collective-permute-done.refs_2_), channel_id=1, source_target_pairs={{0,2},{1,3},{2,0},{3,1},{4,6},{5,7},{6,4},{7,5},{8,10},{9,11},{10,... | collective-permute-start | bytes 3145736 | tf_op jit(solution)/shard_map/ppermute | solution.py:17
  52.0 25.7 %collective-permute-start.7 = (f32[2,14,4,16,128]{4,3,2,1,0:T(8,128)}, f32[2,14,4,16,128]{4,3,2,1,0:T(8,128)S(1)}, u32[]{:S(2)}, u32[]{:S(2)}) collective-permute-start(f32[2,14,4,16,128]{4,3,2,1,0:T(8,128)} %collective-permute-done.1.refs_12_), channel_id=1, source_target_pairs={{0,4},{4,0},{8,12},{12,8},{16,20},{20,16},{24,28},{28,24},{1,5},{5... | collective-permute-start | bytes 2752520 | tf_op jit(solution)/shard_map/ppermute | solution.py:17
  53.7 17.3 %collective-permute-start.5 = (f32[2,7,4,16,128]{4,3,2,1,0:T(8,128)S(1)}, f32[2,7,4,16,128]{4,3,2,1,0:T(8,128)}, u32[]{:S(2)}, u32[]{:S(2)}) collective-permute-start(f32[2,7,4,16,128]{4,3,2,1,0:T(8,128)S(1)} %pad_maximum_fusion.5), channel_id=1, source_target_pairs={{0,8},{4,12},{8,0},{12,4},{16,24},{20,28},{24,16},{28,20},{1,9},{5... | collective-permute-start | bytes 1376264 | tf_op jit(solution)/shard_map/ppermute | solution.py:17
  53.8 25.0 %collective-permute-start.3 = (f32[2,128,1024]{2,1,0:T(8,128)}, f32[2,128,1024]{2,1,0:T(8,128)S(1)}, u32[]{:S(2)}, u32[]{:S(2)}) collective-permute-start(f32[2,128,1024]{2,1,0:T(8,128)} %collective-permute-done.refs_2_), channel_id=1, source_target_pairs={{0,1},{1,0},{2,3},{3,2},{4,5},{5,4},{6,7},{7,6},{8,9},{9,8},{10,11... | collective-permute-start | bytes 3145736 | tf_op jit(solution)/shard_map/ppermute | solution.py:17
  53.9 23.9 %collective-permute-start.6 = (f32[2,7,4,16,128]{4,3,2,1,0:T(8,128)S(1)}, f32[2,7,4,16,128]{4,3,2,1,0:T(8,128)}, u32[]{:S(2)}, u32[]{:S(2)}) collective-permute-start(f32[2,7,4,16,128]{4,3,2,1,0:T(8,128)S(1)} %pad_maximum_fusion.6), channel_id=1, source_target_pairs={{0,16},{4,20},{8,24},{12,28},{16,0},{20,4},{24,8},{28,12},{1,17},{... | collective-permute-start | bytes 1376264 | tf_op jit(solution)/shard_map/ppermute | solution.py:17
  78.7 25.0 %collective-permute-start.8 = (f32[2,128,1024]{2,1,0:T(8,128)}, f32[2,128,1024]{2,1,0:T(8,128)S(1)}, u32[]{:S(2)}, u32[]{:S(2)}) collective-permute-start(f32[2,128,1024]{2,1,0:T(8,128)} %collective-permute-done.4.refs_4_), channel_id=1, source_target_pairs={{0,1},{1,0},{2,3},{3,2},{4,5},{5,4},{6,7},{7,6},{8,9},{9,8},{10,11... | collective-permute-start | bytes 3145736 | tf_op jit(solution)/shard_map/ppermute | solution.py:17
  78.8 21.9 %collective-permute-start.9 = (f32[2,7,4,16,128]{4,3,2,1,0:T(8,128)S(1)}, f32[2,7,4,16,128]{4,3,2,1,0:T(8,128)}, u32[]{:S(2)}, u32[]{:S(2)}) collective-permute-start(f32[2,7,4,16,128]{4,3,2,1,0:T(8,128)S(1)} %pad_maximum_fusion.7), channel_id=1, source_target_pairs={{0,8},{4,12},{8,0},{12,4},{16,24},{20,28},{24,16},{28,20},{1,9},{5... | collective-permute-start | bytes 1376264 | tf_op jit(solution)/shard_map/ppermute | solution.py:17
  78.9 23.9 %collective-permute-start.11 = (f32[2,7,4,16,128]{4,3,2,1,0:T(8,128)S(1)}, f32[2,7,4,16,128]{4,3,2,1,0:T(8,128)}, u32[]{:S(2)}, u32[]{:S(2)}) collective-permute-start(f32[2,7,4,16,128]{4,3,2,1,0:T(8,128)S(1)} %pad_maximum_fusion.8), channel_id=1, source_target_pairs={{0,16},{4,20},{8,24},{12,28},{16,0},{20,4},{24,8},{28,12},{1,17},{... | collective-permute-start | bytes 1376264 | tf_op jit(solution)/shard_map/ppermute | solution.py:17
  81.1 22.2 %collective-permute-start.13 = (f32[2,7,4,16,128]{4,3,2,1,0:T(8,128)}, f32[2,7,4,16,128]{4,3,2,1,0:T(8,128)S(1)}, u32[]{:S(2)}, u32[]{:S(2)}) collective-permute-start(f32[2,7,4,16,128]{4,3,2,1,0:T(8,128)} %collective-permute-done.5.refs_8_), channel_id=1, source_target_pairs={{0,4},{4,0},{8,12},{12,8},{16,20},{20,16},{24,28},{28,24},{1,5},{5... | collective-permute-start | bytes 1376264 | tf_op jit(solution)/shard_map/ppermute | solution.py:17
  81.6 22.1 %collective-permute-start.14 = (f32[2,7,4,16,128]{4,3,2,1,0:T(8,128)}, f32[2,7,4,16,128]{4,3,2,1,0:T(8,128)S(1)}, u32[]{:S(2)}, u32[]{:S(2)}) collective-permute-start(f32[2,7,4,16,128]{4,3,2,1,0:T(8,128)} %collective-permute-done.6.refs_10_), channel_id=1, source_target_pairs={{0,4},{4,0},{8,12},{12,8},{16,20},{20,16},{24,28},{28,24},{1,5},{5... | collective-permute-start | bytes 1376264 | tf_op jit(solution)/shard_map/ppermute | solution.py:17
  100.7 13.6 %collective-permute-start.10 = (f32[2,7,4,16,128]{4,3,2,1,0:T(8,128)}, f32[2,7,4,16,128]{4,3,2,1,0:T(8,128)S(1)}, u32[]{:S(2)}, u32[]{:S(2)}) collective-permute-start(f32[2,7,4,16,128]{4,3,2,1,0:T(8,128)} %collective-permute-done.9.refs_8_), channel_id=1, source_target_pairs={{0,4},{4,0},{8,12},{12,8},{16,20},{20,16},{24,28},{28,24},{1,5},{5... | collective-permute-start | bytes 1376264 | tf_op jit(solution)/shard_map/ppermute | solution.py:17
  102.7 20.4 %collective-permute-start.12 = (f32[2,7,4,16,128]{4,3,2,1,0:T(8,128)}, f32[2,7,4,16,128]{4,3,2,1,0:T(8,128)S(1)}, u32[]{:S(2)}, u32[]{:S(2)}) collective-permute-start(f32[2,7,4,16,128]{4,3,2,1,0:T(8,128)} %collective-permute-done.11.refs_10_), channel_id=1, source_target_pairs={{0,4},{4,0},{8,12},{12,8},{16,20},{20,16},{24,28},{28,24},{1,5},{5... | collective-permute-start | bytes 1376264 | tf_op jit(solution)/shard_map/ppermute | solution.py:17
  123.2 20.7 %collective-permute-start.15 = (f32[4,2,3,4,16,128]{5,4,3,2,1,0:T(8,128)}, f32[4,2,3,4,16,128]{5,4,3,2,1,0:T(8,128)S(1)}, u32[]{:S(2)}, u32[]{:S(2)}) collective-permute-start(f32[4,2,3,4,16,128]{5,4,3,2,1,0:T(8,128)} %get-tuple-element.36), channel_id=1, source_target_pairs={{0,4},{4,0},{8,12},{12,8},{16,20},{20,16},{24,28},{28,24},{1,5},{5... | collective-permute-start | bytes 2359304 | tf_op jit(solution)/shard_map/ppermute | solution.py:17
  136.9 29.4 %collective-permute-start.17 = (f32[4,2,4,4,16,128]{5,4,3,2,1,0:T(8,128)S(1)}, f32[4,2,4,4,16,128]{5,4,3,2,1,0:T(8,128)S(1)}, u32[]{:S(2)}, u32[]{:S(2)}) collective-permute-start(f32[4,2,4,4,16,128]{5,4,3,2,1,0:T(8,128)S(1)} %get-tuple-element.39), channel_id=1, source_target_pairs={{0,4},{4,0},{8,12},{12,8},{16,20},{20,16},{24,28},{28,24},{1,5},{5... | collective-permute-start | bytes 3145736 | tf_op jit(solution)/shard_map/ppermute | solution.py:17
  144.0 24.5 %collective-permute-start.22 = (f32[1,2,2,3,4,16,128]{6,5,4,3,2,1,0:T(8,128)S(1)}, f32[1,2,2,3,4,16,128]{6,5,4,3,2,1,0:T(8,128)S(1)}, u32[]{:S(2)}, u32[]{:S(2)}) collective-permute-start(f32[1,2,2,3,4,16,128]{6,5,4,3,2,1,0:T(8,128)S(1)} %slice_bitcast_fusion.10), channel_id=1, source_target_pairs={{0,16},{4,20},{8,24},{12,28},{16,0},{20,4},{24,8},{28,12},{1,17},{... | collective-permute-start | bytes 1179656 | tf_op jit(solution)/shard_map/ppermute | solution.py:17
  161.5 29.7 %collective-permute-start.24 = (f32[4,2,4,4,16,128]{5,4,3,2,1,0:T(8,128)}, f32[4,2,4,4,16,128]{5,4,3,2,1,0:T(8,128)}, u32[]{:S(2)}, u32[]{:S(2)}) collective-permute-start(f32[4,2,4,4,16,128]{5,4,3,2,1,0:T(8,128)} %get-tuple-element.48), channel_id=1, source_target_pairs={{0,4},{4,0},{8,12},{12,8},{16,20},{20,16},{24,28},{28,24},{1,5},{5... | collective-permute-start | bytes 3145736 | tf_op jit(solution)/shard_map/ppermute | solution.py:17
  167.4 22.5 %collective-permute-start.23 = (f32[1,2,2,4,4,16,128]{6,5,4,3,2,1,0:T(8,128)}, f32[1,2,2,4,4,16,128]{6,5,4,3,2,1,0:T(8,128)}, u32[]{:S(2)}, u32[]{:S(2)}) collective-permute-start(f32[1,2,2,4,4,16,128]{6,5,4,3,2,1,0:T(8,128)} %slice_bitcast_fusion.2), channel_id=1, source_target_pairs={{0,16},{4,20},{8,24},{12,28},{16,0},{20,4},{24,8},{28,12},{1,17},{... | collective-permute-start | bytes 1572872 | tf_op jit(solution)/shard_map/ppermute | solution.py:17
  169.3 12.0 %collective-permute-start.28 = (f32[2,3,4,16,128]{4,3,2,1,0:T(8,128)}, f32[2,3,4,16,128]{4,3,2,1,0:T(8,128)S(1)}, u32[]{:S(2)}, u32[]{:S(2)}) collective-permute-start(f32[2,3,4,16,128]{4,3,2,1,0:T(8,128)} %get-tuple-element.52), channel_id=1, source_target_pairs={{0,8},{4,12},{8,0},{12,4},{16,24},{20,28},{24,16},{28,20},{1,9},{5... | collective-permute-start | bytes 589832 | tf_op jit(solution)/shard_map/ppermute | solution.py:17
  170.9 22.5 %collective-permute-start.19 = (f32[2,128,1024]{2,1,0:T(8,128)}, f32[2,128,1024]{2,1,0:T(8,128)}, u32[]{:S(2)}, u32[]{:S(2)}) collective-permute-start(f32[2,128,1024]{2,1,0:T(8,128)} %get-tuple-element.42), channel_id=1, source_target_pairs={{0,1},{1,0},{2,3},{3,2},{4,5},{5,4},{6,7},{7,6},{8,9},{9,8},{10,11... | collective-permute-start | bytes 3145736 | tf_op jit(solution)/shard_map/ppermute | solution.py:17
  170.9 22.5 %collective-permute-start.16 = (f32[2,128,1024]{2,1,0:T(8,128)}, f32[2,128,1024]{2,1,0:T(8,128)}, u32[]{:S(2)}, u32[]{:S(2)}) collective-permute-start(f32[2,128,1024]{2,1,0:T(8,128)} %get-tuple-element.38), channel_id=1, source_target_pairs={{0,1},{1,0},{2,3},{3,2},{4,5},{5,4},{6,7},{7,6},{8,9},{9,8},{10,11... | collective-permute-start | bytes 3145736 | tf_op jit(solution)/shard_map/ppermute | solution.py:17
  192.7 25.2 %collective-permute-start.25 = (f32[1,2,2,4,4,16,128]{6,5,4,3,2,1,0:T(8,128)S(1)}, f32[1,2,2,4,4,16,128]{6,5,4,3,2,1,0:T(8,128)S(1)}, u32[]{:S(2)}, u32[]{:S(2)}) collective-permute-start(f32[1,2,2,4,4,16,128]{6,5,4,3,2,1,0:T(8,128)S(1)} %slice_bitcast_fusion), channel_id=1, source_target_pairs={{0,16},{4,20},{8,24},{12,28},{16,0},{20,4},{24,8},{28,12},{1,17},{... | collective-permute-start | bytes 1572872 | tf_op jit(solution)/shard_map/ppermute | solution.py:17
  192.8 19.8 %collective-permute-start.26 = (f32[4,2,3,4,16,128]{5,4,3,2,1,0:T(8,128)S(1)}, f32[4,2,3,4,16,128]{5,4,3,2,1,0:T(8,128)S(1)}, u32[]{:S(2)}, u32[]{:S(2)}) collective-permute-start(f32[4,2,3,4,16,128]{5,4,3,2,1,0:T(8,128)S(1)} %copy-done.7), channel_id=1, source_target_pairs={{0,4},{4,0},{8,12},{12,8},{16,20},{20,16},{24,28},{28,24},{1,5},{5... | collective-permute-start | bytes 2359304 | tf_op jit(solution)/shard_map/ppermute | solution.py:17
  194.9 14.8 %collective-permute-start.29 = (f32[2,4,4,16,128]{4,3,2,1,0:T(8,128)S(1)}, f32[2,4,4,16,128]{4,3,2,1,0:T(8,128)S(1)}, u32[]{:S(2)}, u32[]{:S(2)}) collective-permute-start(f32[2,4,4,16,128]{4,3,2,1,0:T(8,128)S(1)} %get-tuple-element.53), channel_id=1, source_target_pairs={{0,8},{4,12},{8,0},{12,4},{16,24},{20,28},{24,16},{28,20},{1,9},{5... | collective-permute-start | bytes 786440 | tf_op jit(solution)/shard_map/ppermute | solution.py:17
  197.5 14.9 %collective-permute-start.20 = (f32[1,128,1024]{2,1,0:T(8,128)S(1)}, f32[1,128,1024]{2,1,0:T(8,128)S(1)}, u32[]{:S(2)}, u32[]{:S(2)}) collective-permute-start(f32[1,128,1024]{2,1,0:T(8,128)S(1)} %slice_bitcast_fusion.4), channel_id=1, source_target_pairs={{0,2},{1,3},{2,0},{3,1},{4,6},{5,7},{6,4},{7,5},{8,10},{9,11},{10,... | collective-permute-start | bytes 1572872 | tf_op jit(solution)/shard_map/ppermute | solution.py:17
  199.8 36.6 %collective-permute-start.18 = (f32[1,128,1024]{2,1,0:T(8,128)S(1)}, f32[1,128,1024]{2,1,0:T(8,128)S(1)}, u32[]{:S(2)}, u32[]{:S(2)}) collective-permute-start(f32[1,128,1024]{2,1,0:T(8,128)S(1)} %slice_bitcast_fusion.6), channel_id=1, source_target_pairs={{0,2},{1,3},{2,0},{3,1},{4,6},{5,7},{6,4},{7,5},{8,10},{9,11},{10,... | collective-permute-start | bytes 1572872 | tf_op jit(solution)/shard_map/ppermute | solution.py:17
  212.5 25.1 %collective-permute-start.21 = (f32[128,1024]{1,0:T(8,128)S(1)}, f32[128,1024]{1,0:T(8,128)S(1)}, u32[]{:S(2)}, u32[]{:S(2)}) collective-permute-start(f32[128,1024]{1,0:T(8,128)S(1)} %fusion.12), channel_id=1, source_target_pairs={{0,8},{4,12},{8,0},{12,4},{16,24},{20,28},{24,16},{28,20},{1,9},{5... | collective-permute-start | bytes 1572872 | tf_op jit(solution)/shard_map/ppermute | solution.py:17
  212.8 20.9 %collective-permute-start.27 = (f32[1,2,2,3,4,16,128]{6,5,4,3,2,1,0:T(8,128)S(1)}, f32[1,2,2,3,4,16,128]{6,5,4,3,2,1,0:T(8,128)S(1)}, u32[]{:S(2)}, u32[]{:S(2)}) collective-permute-start(f32[1,2,2,3,4,16,128]{6,5,4,3,2,1,0:T(8,128)S(1)} %slice_bitcast_fusion.8), channel_id=1, source_target_pairs={{0,16},{4,20},{8,24},{12,28},{16,0},{20,4},{24,8},{28,12},{1,17},{... | collective-permute-start | bytes 1179656 | tf_op jit(solution)/shard_map/ppermute | solution.py:17
  218.1 25.1 %collective-permute-start.30 = (f32[2,4,4,16,128]{4,3,2,1,0:T(8,128)S(1)}, f32[2,4,4,16,128]{4,3,2,1,0:T(8,128)S(1)}, u32[]{:S(2)}, u32[]{:S(2)}) collective-permute-start(f32[2,4,4,16,128]{4,3,2,1,0:T(8,128)S(1)} %get-tuple-element.54), channel_id=1, source_target_pairs={{0,8},{4,12},{8,0},{12,4},{16,24},{20,28},{24,16},{28,20},{1,9},{5... | collective-permute-start | bytes 786440 | tf_op jit(solution)/shard_map/ppermute | solution.py:17
  233.7 13.5 %collective-permute-start.31 = (f32[2,3,4,16,128]{4,3,2,1,0:T(8,128)S(1)}, f32[2,3,4,16,128]{4,3,2,1,0:T(8,128)S(1)}, u32[]{:S(2)}, u32[]{:S(2)}) collective-permute-start(f32[2,3,4,16,128]{4,3,2,1,0:T(8,128)S(1)} %get-tuple-element.78), channel_id=1, source_target_pairs={{0,8},{4,12},{8,0},{12,4},{16,24},{20,28},{24,16},{28,20},{1,9},{5... | collective-permute-start | bytes 589832 | tf_op jit(solution)/shard_map/ppermute | solution.py:17
  (23 other events, 203.7 us)
